TPU v7x, 512 devices: a whole 4x8x8 slice. The times are simulated.
512 devices in a mesh: gz: 32 (over x, y), xy: 16 (over z, core).
Axes of the slice: x: 4, y: 8, z: 8, core: 2. Of those that a mesh axis runs over, the one named last changes fastest.
Arguments:
- features: bfloat16 [64, 128, 64, 128], P(None, 'gz', 'xy'), may hold values from -6 to 6
- conv_w: bfloat16 [64, 64, 3, 3, 3], replicated, may hold values from -0.15625 to 0.15625
- conv_b: float32 [64], replicated, may hold values from -4 to 4
- head_w: bfloat16 [3, 64], replicated, may hold values from -1.796875 to 1.796875
- head_b: float32 [3], replicated, may hold values from -3 to 3
- bins: int32 [128, 64, 128], P('gz', 'xy'), may hold values from 0 to 15
- edge_ids: int32 [3, 128, 64, 128], P(None, 'gz', 'xy'), may hold values from -1 to 4095, as said below
- owner_map: int32 [4096], replicated, may hold values from 0 to 4095, each once
Outputs:
- blended: float32 [3, 128, 64, 128], P(None, 'gz', 'xy')
- edge_hist: float32 [512, 128], P(('gz', 'xy'))
Inputs may be any that keep to these rules, and one draw needn't show every extreme that they name: `edge_ids`: -1 marks a face without contact, among them every face on the volume's last plane along its own axis; every other value is an edge id, 4095 among them.
All inputs are finite; a program needn't handle non-finite values.
Results may differ from a plain program's by a relative error of at most 0.0024.
Values may be sent and summed in bfloat16 or wider, within the bound.
No kernel may reach another device: no remote copies, remote signals or barrier semaphores. Data moves between devices by JAX's collectives and lax.ppermute only.
A program may use at most 64 MiB of HBM per device.

v0:
```python
import jax
import jax.numpy as jnp
from jax import lax
from jax.sharding import PartitionSpec as P

BINS = 16
MARGIN = 2


def padded(array, sides, width):
    for axis, dim in sides:
        peers, length = (lax.axis_size(axis), array.shape[dim])
        up = [(i, (i + 1) % peers) for i in range(peers - 1)]
        down = [(j, i) for i, j in up]
        last = lax.slice_in_dim(array, length - width, length, axis=dim)
        leading = lax.slice_in_dim(array, 0, width, axis=dim)
        before = lax.ppermute(last, axis, up)
        after = lax.ppermute(leading, axis, down)
        array = jnp.concatenate([before, array, after], axis=dim)
    return array


def convolve(source, weights, spacing):
    return lax.conv_general_dilated(
        source[None],
        weights,
        (1, 1, 1),
        spacing,
        dimension_numbers=("NCDHW", "OIDHW", "NCDHW"),
        preferred_element_type=jnp.float32,
    )[0]


def window_weight(cells, extent):
    return jnp.minimum(cells, extent - 1 - cells) + 1.0


def coverage(count, index, total):
    extent = count + 2 * MARGIN
    cells = jnp.arange(count).astype(jnp.float32)
    own = window_weight(cells + MARGIN, extent)
    lower = jnp.where(
        (cells < MARGIN) & (index > 0), window_weight(cells + count + MARGIN, extent), 0.0
    )
    upper = jnp.where(
        (cells >= count - MARGIN) & (index < total - 1),
        window_weight(cells - count + MARGIN, extent),
        0.0,
    )
    return own + lower + upper


def on_device(features, conv_w, conv_b, head_w, head_b, bins, edge_ids, owner_map):
    chans, zcore, ycore, xcells = features.shape
    zext = zcore + 2 * MARGIN
    yext = ycore + 2 * MARGIN
    ext = padded(features, (("gz", 1), ("xy", 2)), MARGIN)
    pre = convolve(ext, conv_w, ((1, 1), (1, 1), (1, 1)))
    hidden = jnp.maximum(pre + conv_b[:, None, None, None], 0.0).astype(jnp.bfloat16)
    logits = jnp.einsum("ac,czyx->azyx", head_w, hidden, preferred_element_type=jnp.float32)
    pred = jax.nn.sigmoid(logits + head_b[:, None, None, None])
    zweight = window_weight(jnp.arange(zext).astype(jnp.float32), zext)
    yweight = window_weight(jnp.arange(yext).astype(jnp.float32), yext)
    weighted = pred * zweight[None, :, None, None] * yweight[None, None, :, None]
    zrims = jnp.concatenate([weighted[:, :MARGIN], weighted[:, zext - MARGIN :]], axis=1)
    zgot = padded(zrims.astype(jnp.bfloat16), (("gz", 1),), MARGIN).astype(zrims.dtype)
    core = weighted[:, MARGIN : MARGIN + zcore]
    core = core.at[:, :MARGIN].add(zgot[:, :MARGIN])
    core = core.at[:, zcore - MARGIN :].add(zgot[:, 3 * MARGIN :])
    yrims = jnp.concatenate([core[:, :, :MARGIN], core[:, :, yext - MARGIN :]], axis=2)
    ygot = padded(yrims, (("xy", 2),), MARGIN)
    center = core[:, :, MARGIN : MARGIN + ycore]
    center = center.at[:, :, :MARGIN].add(ygot[:, :, :MARGIN])
    center = center.at[:, :, ycore - MARGIN :].add(ygot[:, :, 3 * MARGIN :])
    zcover = coverage(zcore, lax.axis_index("gz"), lax.axis_size("gz"))
    ycover = coverage(ycore, lax.axis_index("xy"), lax.axis_size("xy"))
    blended = center / (zcover[:, None] * ycover[None, :])[None, :, :, None]
    valid = edge_ids >= 0
    slots = owner_map[jnp.maximum(edge_ids, 0)]
    index = slots * BINS + bins[None]
    values = jnp.where(valid, blended, 0.0)
    edge_total = owner_map.shape[0]
    table = jax.ops.segment_sum(
        values.reshape(-1), index.reshape(-1), num_segments=edge_total * BINS
    )
    owners = lax.axis_size("gz") * lax.axis_size("xy")
    per_owner = edge_total * BINS // owners
    share = lax.psum_scatter(
        table.reshape(owners, per_owner), ("gz", "xy"), scatter_dimension=0, tiled=True
    )
    return (blended, share)


def solution(mesh):
    in_specs = (
        P(None, "gz", "xy", None),
        P(),
        P(),
        P(),
        P(),
        P("gz", "xy", None),
        P(None, "gz", "xy", None),
        P(),
    )
    out_specs = (P(None, "gz", "xy", None), P(("gz", "xy"), None))
    return jax.shard_map(
        on_device, mesh=mesh, in_specs=in_specs, out_specs=out_specs, check_vma=False
    )
```

profile of v0, /device:TPU:1, one launch (start us, length us, event | category | flops | bytes accessed | tf_op | source)
XLA Modules:
  0.0 422.2 jit_solution(12237642376509510667)
XLA Ops:
  7.2 0.0 copy-start
  7.2 0.0 all-reduce.3.cloned.1.call-start
  7.2 1.4 copy.37
  8.7 0.2 fusion.44
  8.9 4.0 collective-permute-start
  12.9 1.3 collective-permute-start.1
  14.2 0.7 copy_maximum_fusion
  15.0 34.3 %gather_fusion = s32[6144]{0:T(1024)S(1)} fusion(s32[4096]{0:T(1024)S(1)} %copy-done.1, s32[6144]{0:T(1024)S(1)} %broadcast_clamp_fusion), kind=kCustom, calls=%fused_computation | custom fusion | bytes 73728 | tf_op jit(solution)/shard_map/gather | solution.py:79
  49.3 0.0 copy-start.3
  49.3 0.0 collective-permute-done
  49.3 0.0 collective-permute-done.1
  49.3 0.9 pad_maximum_fusion
  50.2 0.9 fusion.43
  51.2 4.8 %collective-permute-start.2 = (bf16[64,8,2,128]{0,2,3,1:T(2,128)(2,1)S(1)}, bf16[64,8,2,128]{0,2,3,1:T(2,128)(2,1)S(1)}, u32[]{:S(2)}, u32[]{:S(2)}) collective-permute-start(bf16[64,8,2,128]{0,2,3,1:T(2,128)(2,1)S(1)} %get-tuple-element.62), channel_id=1, source_target_pairs={{0,1},{1,2},{2,3},{3,4},{4,5},{5,6},{6,7},{7,8},{8,9},{9,10},{10,1... | collective-permute-start | bytes 786440 | tf_op jit(solution)/shard_map/ppermute | solution.py:17
  56.0 2.5 collective-permute-start.3
  58.6 3.5 collective-permute-done.2
  62.1 4.5 %collective-permute-done.3 = bf16[64,8,2,128]{0,2,3,1:T(2,128)(2,1)} collective-permute-done((bf16[64,8,2,128]{0,2,3,1:T(2,128)(2,1)S(1)}, bf16[64,8,2,128]{0,2,3,1:T(2,128)(2,1)}, u32[]{:S(2)}, u32[]{:S(2)}) %collective-permute-start.3) | collective-permute-done | bytes 262176 | tf_op jit(solution)/shard_map/ppermute | solution.py:18
  66.6 3.5 maximum_bitcast_fusion
  70.1 0.0 copy-start.7
  70.1 0.4 pad.8
  70.5 0.3 copy.41
  70.8 0.1 slice.182
  70.9 16.9 %broadcast_select_fusion = f32[8,8,8,17,64]{4,2,3,1,0:T(8,128)S(1)} fusion(pred[8,17]{0,1:T(8,128)(4,1)S(1)} %copy-done.7, bf16[64,64,3,3,3]{1,0,4,3,2:T(8,128)(2,1)S(1)} %copy-done, bf16[64,8,8,1,7,2]{0,4,5,2,1,3:T(8,128)(2,1)S(1)} %slice.182, bf16[64,8,8,1,8,17]{0,4,5,2,1,3:T(8,128)(2,1)S(1)} %copy.41), kind=kOutput, calls=%fused_computation.14 | convolution fusion | flops 1621983232 | bytes 3678344 | tf_op jit(solution)/shard_map/conv_general_dilated | solution.py:24
  87.8 0.0 copy-start.4
  87.8 0.8 copy.42
  88.6 0.0 copy-start.6
  88.6 0.0 copy-done.4
  88.6 0.0 copy-start.5
  88.7 0.0 copy-start.2
  88.7 0.4 fusion.3
  89.1 0.2 copy-done.6
  89.3 0.6 fusion.11
  89.9 0.1 fusion.41
  90.1 4.3 %collective-permute-start.4 = (bf16[3,2,8,128]{3,2,0,1:T(8,128)(2,1)S(1)}, bf16[3,2,8,128]{3,2,0,1:T(8,128)(2,1)S(1)}, u32[]{:S(2)}, u32[]{:S(2)}) collective-permute-start(bf16[3,2,8,128]{3,2,0,1:T(8,128)(2,1)S(1)} %get-tuple-element.68), channel_id=1, source_target_pairs={{0,16},{16,32},{32,48},{48,64},{64,80},{80,96},{96,112},{112,128},... | collective-permute-start | bytes 36872 | tf_op jit(solution)/shard_map/ppermute | solution.py:17
  94.4 1.3 collective-permute-start.5
  95.7 0.0 collective-permute-done.4
  95.7 3.1 collective-permute-done.5
  98.8 3.1 collective-permute-start.6
  101.9 0.1 broadcast_multiply_fusion.1
  102.0 1.9 collective-permute-start.7
  103.9 0.0 collective-permute-done.6
  103.9 3.1 collective-permute-done.7
  107.0 0.1 compare_select_fusion
  107.1 33.2 %scatter_custom_fusion = f32[65536]{0:T(1024)} fusion(s32[6144]{0:T(1024)S(1)} %bitcast.41, f32[6144]{0:T(1024)S(1)} %bitcast.42, f32[]{:T(128)} %constant.132.clone.1), kind=kCustom, calls=%fused_computation.20 | custom fusion | flops 6144 | bytes 262148 | tf_op jit(solution)/shard_map/scatter-add | solution.py:83
  140.4 0.0 all-reduce.3.cloned.1.call-update
  140.4 0.6 copy.49
  141.0 273.1 %all-reduce.3.cloned.1.call-done = f32[512,128]{1,0:T(8,128)} async-done(((f32[512,128]{1,0:T(8,128)}), f32[512,128]{1,0:T(8,128)}) %all-reduce.3.cloned.1.call-update) | async-done | bytes 262160
  414.1 1.2 constant_dynamic-slice_fusion
  (22 shorter events, 0.1 us)
Async XLA Ops:
  7.2 63.8 %copy-start = (bf16[64,64,3,3,3]{1,0,4,3,2:T(8,128)(2,1)S(1)}, bf16[64,64,3,3,3]{1,0,4,3,2:T(8,128)(2,1)}, u32[]{:S(2)}) copy-start(bf16[64,64,3,3,3]{1,0,4,3,2:T(8,128)(2,1)} %param.17) | copy-start | bytes 663556
  7.2 7.8 %copy-start.1 = (s32[4096]{0:T(1024)S(1)}, s32[4096]{0:T(1024)}, u32[]{:S(2)}) copy-start(s32[4096]{0:T(1024)} %param.23) | copy-start | bytes 49156
  7.2 406.9 %all-reduce.3.cloned.1.call-start = ((), (), s32[]{:S(2)}) async-start(), calls=%async_computation | async-start | bytes 524288
  8.9 40.5 %collective-permute-start = (bf16[64,2,4,128]{0,2,3,1:T(4,128)(2,1)S(1)}, bf16[64,2,4,128]{0,2,3,1:T(4,128)(2,1)S(1)}, u32[]{:S(2)}, u32[]{:S(2)}) collective-permute-start(bf16[64,2,4,128]{0,2,3,1:T(4,128)(2,1)S(1)} %get-tuple-element.64), channel_id=1, source_target_pairs={{0,16},{16,32},{32,48},{48,64},{64,80},{80,96},{96,112},{112,128},... | collective-permute-start | bytes 393224 | tf_op jit(solution)/shard_map/ppermute | solution.py:17
  12.9 36.4 %collective-permute-start.1 = (bf16[64,2,4,128]{0,2,3,1:T(4,128)(2,1)S(1)}, bf16[64,2,4,128]{0,2,3,1:T(4,128)(2,1)S(1)}, u32[]{:S(2)}, u32[]{:S(2)}) collective-permute-start(bf16[64,2,4,128]{0,2,3,1:T(4,128)(2,1)S(1)} %get-tuple-element.65), channel_id=1, source_target_pairs={{16,0},{32,16},{48,32},{64,48},{80,64},{96,80},{112,96},{128,112},... | collective-permute-start | bytes 393224 | tf_op jit(solution)/shard_map/ppermute | solution.py:18
  49.3 9.3 %copy-start.3 = (s32[4,4,128]{2,1,0:T(4,128)S(1)}, s32[4,4,128]{2,1,0:T(4,128)}, u32[]{:S(2)}) copy-start(s32[4,4,128]{2,1,0:T(4,128)} %param.21) | copy-start | bytes 24580
  51.2 11.0 %collective-permute-start.2 = (bf16[64,8,2,128]{0,2,3,1:T(2,128)(2,1)S(1)}, bf16[64,8,2,128]{0,2,3,1:T(2,128)(2,1)S(1)}, u32[]{:S(2)}, u32[]{:S(2)}) collective-permute-start(bf16[64,8,2,128]{0,2,3,1:T(2,128)(2,1)S(1)} %get-tuple-element.62), channel_id=1, source_target_pairs={{0,1},{1,2},{2,3},{3,4},{4,5},{5,6},{6,7},{7,8},{8,9},{9,10},{10,1... | collective-permute-start | bytes 786440 | tf_op jit(solution)/shard_map/ppermute | solution.py:17
  56.0 10.6 %collective-permute-start.3 = (bf16[64,8,2,128]{0,2,3,1:T(2,128)(2,1)S(1)}, bf16[64,8,2,128]{0,2,3,1:T(2,128)(2,1)}, u32[]{:S(2)}, u32[]{:S(2)}) collective-permute-start(bf16[64,8,2,128]{0,2,3,1:T(2,128)(2,1)S(1)} %get-tuple-element.63), channel_id=1, source_target_pairs={{1,0},{2,1},{3,2},{4,3},{5,4},{6,5},{7,6},{8,7},{9,8},{10,9},{11,1... | collective-permute-start | bytes 786440 | tf_op jit(solution)/shard_map/ppermute | solution.py:18
  70.1 0.8 copy-start.7
  87.8 0.8 copy-start.4
  88.6 0.7 copy-start.6
  88.6 1.3 copy-start.5
  88.7 18.4 %copy-start.2 = (s32[3,4,4,128]{3,2,1,0:T(4,128)S(1)}, s32[3,4,4,128]{3,2,1,0:T(4,128)}, u32[]{:S(2)}) copy-start(s32[3,4,4,128]{3,2,1,0:T(4,128)} %param.22) | copy-start | bytes 73732
  90.1 5.6 %collective-permute-start.4 = (bf16[3,2,8,128]{3,2,0,1:T(8,128)(2,1)S(1)}, bf16[3,2,8,128]{3,2,0,1:T(8,128)(2,1)S(1)}, u32[]{:S(2)}, u32[]{:S(2)}) collective-permute-start(bf16[3,2,8,128]{3,2,0,1:T(8,128)(2,1)S(1)} %get-tuple-element.68), channel_id=1, source_target_pairs={{0,16},{16,32},{32,48},{48,64},{64,80},{80,96},{96,112},{112,128},... | collective-permute-start | bytes 36872 | tf_op jit(solution)/shard_map/ppermute | solution.py:17
  94.4 4.4 %collective-permute-start.5 = (bf16[3,2,8,128]{3,2,0,1:T(8,128)(2,1)S(1)}, bf16[3,2,8,128]{3,2,0,1:T(8,128)(2,1)S(1)}, u32[]{:S(2)}, u32[]{:S(2)}) collective-permute-start(bf16[3,2,8,128]{3,2,0,1:T(8,128)(2,1)S(1)} %get-tuple-element.69), channel_id=1, source_target_pairs={{16,0},{32,16},{48,32},{64,48},{80,64},{96,80},{112,96},{128,112},... | collective-permute-start | bytes 36872 | tf_op jit(solution)/shard_map/ppermute | solution.py:18
  98.8 5.1 %collective-permute-start.6 = (f32[3,4,2,128]{3,2,0,1:T(2,128)S(1)}, f32[3,4,2,128]{3,2,0,1:T(2,128)S(1)}, u32[]{:S(2)}, u32[]{:S(2)}) collective-permute-start(f32[3,4,2,128]{3,2,0,1:T(2,128)S(1)} %get-tuple-element.67), channel_id=1, source_target_pairs={{0,1},{1,2},{2,3},{3,4},{4,5},{5,6},{6,7},{7,8},{8,9},{9,10},{10,1... | collective-permute-start | bytes 36872 | tf_op jit(solution)/shard_map/ppermute | solution.py:17
  102.0 5.0 %collective-permute-start.7 = (f32[3,4,2,128]{3,2,0,1:T(2,128)S(1)}, f32[3,4,2,128]{3,2,0,1:T(2,128)S(1)}, u32[]{:S(2)}, u32[]{:S(2)}) collective-permute-start(f32[3,4,2,128]{3,2,0,1:T(2,128)S(1)} %get-tuple-element.66), channel_id=1, source_target_pairs={{1,0},{2,1},{3,2},{4,3},{5,4},{6,5},{7,6},{8,7},{9,8},{10,9},{11,1... | collective-permute-start | bytes 36872 | tf_op jit(solution)/shard_map/ppermute | solution.py:18
Sparse Core Ops, SparseCore 0:
  140.5 273.5 all-reduce.2
where the time goes:
time: 423 us; the launch traced here: 422 us
  waiting for transfers between devices  287 us (68%)
  local copies, waits for them, and re-layouts  40.5 us (10%)
  other arithmetic  39.1 us (9%)
  starting transfers between devices  23.3 us (6%)
  matrix products  17.5 us (4%)
  between operations  14.4 us (3%)
    unnamed x2, waiting for transfers between devices  273 us
    gather x1, local copies, waits for them, and re-layouts, on_device(): slots = owner_map[jnp.maximum(edge_ids, 0)]  34.3 us
    scatter-add x1, other arithmetic, on_device(): jax.ops.segment_sum(values.reshape(-1), index.reshape(-1), num_segments=e...  33.2 us
    conv_general_dilated x1, matrix products, convolve(): lax.conv_general_dilated(source[None], weights, (1, 1, 1), spacing, dimen...  16.9 us
    ppermute x4, starting transfers between devices, padded(): before = lax.ppermute(last, axis, up)  16.2 us
    ppermute x4, waiting for transfers between devices, padded(): after = lax.ppermute(leading, axis, down)  10.6 us
  transfers between devices with their start and end apart: 9, of which 5 were waited for; matrix products, arithmetic and copies ran while one was open for 8% of the time, Pallas kernels for 0%

commit v1 on v0

v1 whole, which is shorter than its diff:
```python
import jax
import jax.numpy as jnp
from jax import lax
from jax.experimental import pallas as pl
from jax.experimental.pallas import tpu as pltpu
from jax.sharding import PartitionSpec as P

BINS = 16
CORE = 4
TAPS = 3
VMEM_LIMIT = 48 * 1024 * 1024

VARIANTS = (
    (0, (0, 1, 2)),
    (1, (0, 1, 2)),
    (1, (0, 1)),
    (2, (1, 2)),
    (2, (0, 1, 2)),
    (3, (0, 1, 2)),
)


def neighbours(axis, first, last):
    peers = lax.axis_size(axis)
    up = [(i, i + 1) for i in range(peers - 1)]
    down = [(j, i) for i, j in up]
    return lax.ppermute(last, axis, up), lax.ppermute(first, axis, down)


def variant_weights(index, total):
    lower = jnp.where(index > 0, 1.0, 0.0)
    upper = jnp.where(index < total - 1, 1.0, 0.0)
    weights = (3.0 + 2.0 * lower, 4.0, lower, upper, 4.0, 3.0 + 2.0 * upper)
    cover = (3.0 + 2.0 * lower, 4.0 + lower, 4.0 + upper, 3.0 + 2.0 * upper)
    return weights, cover


def prepare_kernel(peers, ids_ref, bins_ref, map_ref, taps_ref, row_ref, col_ref, w_ref):
    ids = jnp.maximum(ids_ref[...], 0)
    table = map_ref[...]
    halves = jnp.concatenate([table // 64, table % 64], axis=0).astype(jnp.float32).astype(jnp.bfloat16)
    which = lax.broadcasted_iota(jnp.int32, (64, 128), 0)
    for r in range(ids.shape[0]):
        one = ids[r : r + 1]
        high = jnp.where(one // 64 == which, 1.0, 0.0).astype(jnp.bfloat16)
        found = lax.dot_general(halves, high, (((1,), (0,)), ((), ())), preferred_element_type=jnp.float32)
        low = one % 64 == which
        upper = jnp.sum(jnp.where(low, found[:64], 0.0), axis=0, keepdims=True)
        lower = jnp.sum(jnp.where(low, found[64:], 0.0), axis=0, keepdims=True)
        slot = upper.astype(jnp.int32) * 64 + lower.astype(jnp.int32)
        owner = slot // 8
        row_ref[r : r + 1] = owner
        col_ref[r : r + 1] = slot % 8 * BINS + bins_ref[r % 16 : r % 16 + 1]
    for dx in range(TAPS):
        rows = jnp.concatenate([taps_ref[t // 3, t % 3, dx] for t in range(9)], axis=1)
        w_ref[64 * dx : 64 * dx + 64, :576] = rows
        w_ref[64 * dx : 64 * dx + 64, 640:1024] = rows[:, 192:]


def main_kernel(
    f_ref, zlo_ref, zhi_ref, ylo_ref, yhi_ref, w_ref, cb_ref, hw_ref, hb_ref, wz_ref, ids_ref, row_ref, col_ref,
    out_ref, table_ref, g_ref, a_ref, b_ref,
):
    zero = jnp.zeros((64, 128), jnp.bfloat16)

    def cell(z, y):
        if y == 0:
            return ylo_ref[z, 0]
        if y == 5:
            return yhi_ref[z, 0]
        if z == 0:
            return zlo_ref[0, y - 1]
        if z == 5:
            return zhi_ref[0, y - 1]
        return f_ref[z - 1, y - 1]

    for z in range(6):
        for dy in range(TAPS):
            for v, (y, kept) in enumerate(VARIANTS):
                part = cell(z, y + dy) if dy in kept else zero
                g_ref[(z * 3 + dy) * 64 : (z * 3 + dy) * 64 + 64, v * 128 : v * 128 + 128] = part

    lane = lax.broadcasted_iota(jnp.int32, (64, 128), 1)
    bias = cb_ref[...]
    head_b = hb_ref[...]
    head_w = hw_ref[...]
    preds = {}
    for zv, (z, kept) in enumerate(VARIANTS):
        w = w_ref[:, :576] if len(kept) == 3 else (w_ref[:, :384] if kept[0] == 0 else w_ref[:, 640:1024])
        first = (z + kept[0]) * 192
        for pair in range(3):
            g = g_ref[first : first + 192 * len(kept), pair * 256 : pair * 256 + 256]
            p = lax.dot_general(w, g, (((1,), (0,)), ((), ())), preferred_element_type=jnp.float32)
            hidden = []
            for half in range(2):
                q = p[:, half * 128 : half * 128 + 128]
                before = jnp.where(lane == 0, 0.0, pltpu.roll(q[:64], 1, 1))
                after = jnp.where(lane == 127, 0.0, pltpu.roll(q[128:], 127, 1))
                pre = before + q[64:128] + after
                hidden.append(jnp.maximum(pre + bias, 0.0).astype(jnp.bfloat16))
            logits = lax.dot_general(
                head_w, jnp.concatenate(hidden, axis=1), (((1,), (0,)), ((), ())), preferred_element_type=jnp.float32
            )
            for half in range(2):
                preds[zv, pair * 2 + half] = jax.nn.sigmoid(logits[:, half * 128 : half * 128 + 128] + head_b)

    blends = {}
    for z in range(CORE):
        for y in range(CORE):
            total = None
            for zv, (zc, _) in enumerate(VARIANTS):
                for yv, (yc, _) in enumerate(VARIANTS):
                    if (zc, yc) == (z, y):
                        term = preds[zv, yv] * (wz_ref[0, zv] * wz_ref[1, yv])
                        total = term if total is None else total + term
            blends[z * CORE + y] = total / (wz_ref[2, z] * wz_ref[2, 4 + y])
    for a in range(3):
        for zy in range(16):
            out_ref[a * 16 + zy : a * 16 + zy + 1, :] = blends[zy][a : a + 1]

    owner = lax.broadcasted_iota(jnp.int32, (256, 128), 0).astype(jnp.float32).astype(jnp.bfloat16)
    column = owner[:128]
    one = jnp.ones((), jnp.bfloat16)
    none = jnp.zeros((), jnp.bfloat16)
    for r in range(48):
        value = jnp.where(ids_ref[r : r + 1] >= 0, out_ref[r : r + 1], 0.0)
        big = value.astype(jnp.bfloat16)
        small = (value - big.astype(jnp.float32)).astype(jnp.bfloat16)
        row = row_ref[r : r + 1].astype(jnp.float32)
        col = col_ref[r : r + 1].astype(jnp.float32).astype(jnp.bfloat16)
        lanes = slice(r * 128, r * 128 + 128)
        a_ref[:256, lanes] = jnp.where(owner == row.astype(jnp.bfloat16), one, none)
        a_ref[256:, lanes] = jnp.where(owner == (row - 256.0).astype(jnp.bfloat16), one, none)
        here = column == col
        b_ref[:128, lanes] = jnp.where(here, big, none)
        b_ref[128:, lanes] = jnp.where(here, small, none)
    both = lax.dot_general(
        a_ref[...], b_ref[...], (((1,), (1,)), ((), ())), preferred_element_type=jnp.float32
    )
    table_ref[...] = (both[:, :128] + both[:, 128:]).astype(jnp.bfloat16)


def vmem(count):
    return [pl.BlockSpec(memory_space=pltpu.VMEM)] * count


def on_device(features, conv_w, conv_b, head_w, head_b, bins, edge_ids, owner_map):
    gz_peers, xy_peers = lax.axis_size("gz"), lax.axis_size("xy")
    cells = jnp.transpose(features, (1, 2, 0, 3))
    zlo, zhi = neighbours("gz", cells[:1], cells[CORE - 1 :])
    ids = edge_ids.reshape(48, 128)
    rows, cols, weights = pl.pallas_call(
        lambda *refs: prepare_kernel(xy_peers, *refs),
        out_shape=(
            jax.ShapeDtypeStruct((48, 128), jnp.int32),
            jax.ShapeDtypeStruct((48, 128), jnp.int32),
            jax.ShapeDtypeStruct((192, 1024), jnp.bfloat16),
        ),
        in_specs=vmem(4),
        out_specs=tuple(vmem(3)),
        compiler_params=pltpu.CompilerParams(vmem_limit_bytes=VMEM_LIMIT),
        name="prepare",
    )(ids, bins.reshape(16, 128), owner_map.reshape(64, 64).T, jnp.transpose(conv_w, (2, 3, 4, 0, 1)))
    first = jnp.concatenate([zlo[:, :1], cells[:, :1], zhi[:, :1]], axis=0)
    last = jnp.concatenate([zlo[:, CORE - 1 :], cells[:, CORE - 1 :], zhi[:, CORE - 1 :]], axis=0)
    ylo, yhi = neighbours("xy", first, last)
    zweights, zcover = variant_weights(lax.axis_index("gz"), gz_peers)
    yweights, ycover = variant_weights(lax.axis_index("xy"), xy_peers)
    blank = (0.0,) * 2
    scalars = jnp.stack(
        [jnp.stack([jnp.asarray(v, jnp.float32) for v in line]) for line in (zweights + blank, yweights + blank, zcover + ycover)]
    )
    blended, table = pl.pallas_call(
        main_kernel,
        out_shape=(
            jax.ShapeDtypeStruct((48, 128), jnp.float32),
            jax.ShapeDtypeStruct((512, 128), jnp.bfloat16),
        ),
        in_specs=vmem(9) + [pl.BlockSpec(memory_space=pltpu.SMEM)] + vmem(3),
        out_specs=tuple(vmem(2)),
        scratch_shapes=[
            pltpu.VMEM((6 * 192, 768), jnp.bfloat16),
            pltpu.VMEM((512, 48 * 128), jnp.bfloat16),
            pltpu.VMEM((256, 48 * 128), jnp.bfloat16),
        ],
        compiler_params=pltpu.CompilerParams(vmem_limit_bytes=VMEM_LIMIT),
        name="blend_and_count",
    )(
        cells, zlo, zhi, ylo, yhi, weights, conv_b.reshape(64, 1),
        jnp.pad(head_w, ((0, 5), (0, 0))), jnp.pad(head_b, (0, 5)).reshape(8, 1), scalars, ids, rows, cols,
    )
    parts = lax.all_to_all(table.reshape(gz_peers, xy_peers, 128), "gz", 0, 0, tiled=True)
    sums = jnp.sum(parts.astype(jnp.float32), axis=0)
    share = jnp.sum(lax.all_to_all(sums, "xy", 0, 0, tiled=True), axis=0, keepdims=True)
    return blended.reshape(3, CORE, CORE, 128), share


def solution(mesh):
    in_specs = (
        P(None, "gz", "xy", None),
        P(),
        P(),
        P(),
        P(),
        P("gz", "xy", None),
        P(None, "gz", "xy", None),
        P(),
    )
    out_specs = (P(None, "gz", "xy", None), P(("gz", "xy"), None))
    return jax.shard_map(
        on_device, mesh=mesh, in_specs=in_specs, out_specs=out_specs, check_vma=False
    )
```

time: 423 us -> 69.1 us (0.16)
  waiting for transfers between devices: 287 us -> 1.22 us
  other arithmetic: 39.1 us -> 0.62 us
  blocking collectives: 0 us -> 36.9 us
  local copies, waits for them, and re-layouts: 40.5 us -> 4.79 us
  matrix products: 17.5 us -> 0 us
  between operations: 14.4 us -> 0.83 us
  Pallas kernels: 0 us -> 8.25 us
  starting transfers between devices: 23.3 us -> 16.1 us
    unnamed x2 -> x0, waiting for transfers between devices: 273 us -> none
    all_to_all x0 -> x2, blocking collectives: none -> 36.9 us  [the longest x1 18.8 us: on_device(): lax.all_to_all(table.reshape(gz_peers, xy_peers, 128), 'gz', 0, 0, tiled=...]
    gather x1 -> x0, local copies, waits for them, and re-layouts: 34.3 us -> none  [on_device(): slots = owner_map[jnp.maximum(edge_ids, 0)]]
    scatter-add x5 -> x0, other arithmetic: 33.3 us -> none  [the longest x1 33.2 us: on_device(): jax.ops.segment_sum(values.reshape(-1), index.reshape(-1), num_segments=e...]
    conv_general_dilated x1 -> x0, matrix products: 16.9 us -> none  [convolve(): lax.conv_general_dilated(source[None], weights, (1, 1, 1), spacing, dimen...]
    ppermute x8 -> x4, waiting for transfers between devices: 14.2 us -> 1.22 us  [neighbours(): return (lax.ppermute(last, axis, up), lax.ppermute(first, axis, down))]
    pallas_call x0 -> x2, Pallas kernels: none -> 8.25 us  [the longest x1 7.2 us: on_device(): pl.pallas_call(main_kernel, out_shape=(jax.ShapeDtypeStruct((48, 128), jn...]
    ppermute x8 -> x4, starting transfers between devices: 23.3 us -> 16.1 us  [neighbours(): return (lax.ppermute(last, axis, up), lax.ppermute(first, axis, down))]
  transfers between devices with their start and end apart: 9 -> 4, of which waited for: 5 -> 1; matrix products, arithmetic and copies ran while one was open for 8% -> 1% of each run, Pallas kernels for 0% -> 2%
where the time goes in v1:
time: 69.1 us; the launch traced here: 68.7 us
  blocking collectives  36.9 us (53%)
  starting transfers between devices  16.1 us (23%)
  Pallas kernels  8.25 us (12%)
  local copies, waits for them, and re-layouts  4.79 us (7%)
  waiting for transfers between devices  1.22 us (2%)
  between operations  0.83 us (1%)
    all_to_all x1, blocking collectives, on_device(): lax.all_to_all(table.reshape(gz_peers, xy_peers, 128), 'gz', 0, 0, tiled=...  18.8 us
    all_to_all x1, blocking collectives, on_device(): lax.all_to_all(sums, 'xy', 0, 0, tiled=True)  18.2 us
    ppermute x4, starting transfers between devices, neighbours(): return (lax.ppermute(last, axis, up), lax.ppermute(first, axis, down))  16.1 us
    pallas_call x1, Pallas kernels, on_device(): pl.pallas_call(main_kernel, out_shape=(jax.ShapeDtypeStruct((48, 128), jn...  7.2 us
    unnamed x15, local copies, waits for them, and re-layouts  4.17 us
  transfers between devices with their start and end apart: 4, of which 1 were waited for; matrix products, arithmetic and copies ran while one was open for 1% of the time, Pallas kernels for 2%

profile of v1, /device:TPU:1, one launch (start us, length us, event | category | flops | bytes accessed | tf_op | source)
XLA Modules:
  0.0 68.7 jit_solution(5138946055249364789)
XLA Ops:
  0.6 1.0 %copy.22 = bf16[64,4,4,128]{3,0,2,1:T(8,128)(2,1)S(1)} copy(bf16[64,4,4,128]{3,2,1,0:T(4,128)(2,1)} %param.8) | data formatting | bytes 524288 | tf_op args[0]
  1.7 0.0 copy-start
  1.7 1.4 %collective-permute-start.1 = (bf16[1,4,64,128]{3,2,1,0:T(8,128)(2,1)S(1)}, bf16[1,4,64,128]{3,2,1,0:T(8,128)(2,1)S(1)}, u32[]{:S(2)}, u32[]{:S(2)}) collective-permute-start(bf16[1,4,64,128]{3,2,1,0:T(8,128)(2,1)S(1)} %get-tuple-element.14), channel_id=1, source_target_pairs={{16,0},{32,16},{48,32},{64,48},{80,64},{96,80},{112,96},{128,112},... | collective-permute-start | bytes 196616 | tf_op jit(solution)/shard_map/ppermute | solution.py:27
  3.1 4.7 %collective-permute-start = (bf16[1,4,64,128]{3,2,1,0:T(8,128)(2,1)S(1)}, bf16[1,4,64,128]{3,2,1,0:T(8,128)(2,1)S(1)}, u32[]{:S(2)}, u32[]{:S(2)}) collective-permute-start(bf16[1,4,64,128]{3,2,1,0:T(8,128)(2,1)S(1)} %get-tuple-element.15), channel_id=1, source_target_pairs={{0,16},{16,32},{32,48},{48,64},{64,80},{80,96},{96,112},{112,128},... | collective-permute-start | bytes 196616 | tf_op jit(solution)/shard_map/ppermute | solution.py:27
  7.8 0.0 copy-start.6
  7.9 0.6 copy-done.6
  8.5 0.1 copy.20.hb_ref
  8.6 0.0 copy-start.5
  8.6 0.7 copy-done.5
  9.2 0.0 copy-start.3
  9.2 0.1 copy.19.cb_ref
  9.3 0.6 copy-done.3
  10.0 0.1 reshape.29
  10.0 0.0 copy-start.4
  10.0 0.1 copy.18
  10.1 0.6 copy-done.4
  10.7 0.0 copy-start.1
  10.7 0.1 stack.71
  10.8 0.1 stack.65
  10.9 0.0 copy-start.2
  10.9 0.1 stack.77
  11.0 0.0 copy-done
  11.0 0.5 copy-done.1
  11.5 0.1 copy-done.2
  11.6 1.0 %prepare.1 = (s32[48,128]{1,0:T(8,128)S(1)}, s32[48,128]{1,0:T(8,128)S(1)}, bf16[192,1024]{1,0:T(8,128)(2,1)S(1)}) custom-call(s32[48,128]{1,0:T(8,128)S(1)} %bitcast.35, s32[16,128]{1,0:T(8,128)S(1)} %bitcast.37, s32[64,64]{1,0:T(8,128)S(1)} %bitcast.33, bf16[3,3,3,64,64]{4,3,2,1,0:T(8,128)(2,1)S(1)} %bitcast.32), custom_call_target="tpu_custom_call" | custom-call | tf_op jit(solution)/shard_map/prepare/pallas_call | solution.py:152
  12.7 0.0 collective-permute-done.1.zhi_ref
  12.7 0.0 collective-permute-done.zlo_ref
  12.7 5.3 %collective-permute-start.2 = (bf16[6,1,64,128]{3,2,1,0:T(8,128)(2,1)S(1)}, bf16[6,1,64,128]{3,2,1,0:T(8,128)(2,1)S(1)}, u32[]{:S(2)}, u32[]{:S(2)}) collective-permute-start(bf16[6,1,64,128]{3,2,1,0:T(8,128)(2,1)S(1)} %pad_maximum_fusion), channel_id=1, source_target_pairs={{0,1},{1,2},{2,3},{3,4},{4,5},{5,6},{6,7},{7,8},{8,9},{9,10},{10,1... | collective-permute-start | bytes 294920 | tf_op jit(solution)/shard_map/ppermute | solution.py:27
  18.0 4.7 %collective-permute-start.3 = (bf16[6,1,64,128]{3,2,1,0:T(8,128)(2,1)S(1)}, bf16[6,1,64,128]{3,2,1,0:T(8,128)(2,1)S(1)}, u32[]{:S(2)}, u32[]{:S(2)}) collective-permute-start(bf16[6,1,64,128]{3,2,1,0:T(8,128)(2,1)S(1)} %pad_maximum_fusion.1), channel_id=1, source_target_pairs={{1,0},{2,1},{3,2},{4,3},{5,4},{6,5},{7,6},{8,7},{9,8},{10,9},{11,1... | collective-permute-start | bytes 294920 | tf_op jit(solution)/shard_map/ppermute | solution.py:27
  22.8 0.0 collective-permute-done.2.ylo_ref
  22.8 1.2 %collective-permute-done.3.yhi_ref = bf16[6,1,64,128]{3,2,1,0:T(8,128)(2,1)S(1)} collective-permute-done((bf16[6,1,64,128]{3,2,1,0:T(8,128)(2,1)S(1)}, bf16[6,1,64,128]{3,2,1,0:T(8,128)(2,1)S(1)}, u32[]{:S(2)}, u32[]{:S(2)}) %collective-permute-start.3) | collective-permute-done | bytes 98336 | tf_op jit(solution)/shard_map/ppermute | solution.py:27
  24.0 7.2 %blend_and_count.1 = (f32[48,128]{1,0:T(8,128)}, bf16[512,128]{1,0:T(8,128)(2,1)S(1)}) custom-call(bf16[4,4,64,128]{3,2,1,0:T(8,128)(2,1)S(1)} %bitcast.31, bf16[1,4,64,128]{3,2,1,0:T(8,128)(2,1)S(1)} %collective-permute-done.zlo_ref, bf16[1,4,64,128]{3,2,1,0:T(8,128)(2,1)S(1)} %collective-permute-done.1.zhi_ref, ...), custom_call_target="tpu_custom_call" | custom-call | tf_op jit(solution)/shard_map/blend_and_count/pallas_call | solution.py:173
  31.2 18.8 %all_to_all.14 = bf16[32,16,128]{2,1,0:T(8,128)(2,1)S(1)} all-to-all(bf16[32,16,128]{2,1,0:T(8,128)(2,1)S(1)} %bitcast.34), channel_id=1, replica_groups=mesh['gz'=32,'xy'=16] {'gz'}, dimensions={0} | all-to-all | bytes 262144 | tf_op jit(solution)/shard_map/all_to_all | solution.py:192
  50.0 18.2 %all_to_all.15 = f32[16,1,128]{2,1,0:T(1,128)S(1)} all-to-all(f32[16,1,128]{2,1,0:T(1,128)S(1)} %bitcast.38), channel_id=1, replica_groups=mesh['gz'=32,'xy'=16] {'xy'}, dimensions={0} | all-to-all | bytes 16384 | tf_op jit(solution)/shard_map/all_to_all | solution.py:194
  68.1 0.5 reduce_sum.19
  (11 shorter events, 0.1 us)
Async XLA Ops:
  1.7 9.3 %copy-start = (bf16[64,64,3,3,3]{1,0,4,3,2:T(8,128)(2,1)S(1)}, bf16[64,64,3,3,3]{1,0,4,3,2:T(8,128)(2,1)}, u32[]{:S(2)}) copy-start(bf16[64,64,3,3,3]{1,0,4,3,2:T(8,128)(2,1)} %param.9) | copy-start | bytes 663556
  1.7 11.0 %collective-permute-start.1 = (bf16[1,4,64,128]{3,2,1,0:T(8,128)(2,1)S(1)}, bf16[1,4,64,128]{3,2,1,0:T(8,128)(2,1)S(1)}, u32[]{:S(2)}, u32[]{:S(2)}) collective-permute-start(bf16[1,4,64,128]{3,2,1,0:T(8,128)(2,1)S(1)} %get-tuple-element.14), channel_id=1, source_target_pairs={{16,0},{32,16},{48,32},{64,48},{80,64},{96,80},{112,96},{128,112},... | collective-permute-start | bytes 196616 | tf_op jit(solution)/shard_map/ppermute | solution.py:27
  3.1 9.6 %collective-permute-start = (bf16[1,4,64,128]{3,2,1,0:T(8,128)(2,1)S(1)}, bf16[1,4,64,128]{3,2,1,0:T(8,128)(2,1)S(1)}, u32[]{:S(2)}, u32[]{:S(2)}) collective-permute-start(bf16[1,4,64,128]{3,2,1,0:T(8,128)(2,1)S(1)} %get-tuple-element.15), channel_id=1, source_target_pairs={{0,16},{16,32},{32,48},{48,64},{64,80},{80,96},{96,112},{112,128},... | collective-permute-start | bytes 196616 | tf_op jit(solution)/shard_map/ppermute | solution.py:27
  7.8 0.7 copy-start.6
  8.6 0.7 copy-start.5
  9.2 0.7 %copy-start.3 = (s32[4096]{0:T(1024)S(1)}, s32[4096]{0:T(1024)}, u32[]{:S(2)}) copy-start(s32[4096]{0:T(1024)} %param.15) | copy-start | bytes 49156
  10.0 0.7 copy-start.4
  10.7 0.7 %copy-start.1 = (s32[3,4,4,128]{3,2,1,0:T(4,128)S(1)}, s32[3,4,4,128]{3,2,1,0:T(4,128)}, u32[]{:S(2)}) copy-start(s32[3,4,4,128]{3,2,1,0:T(4,128)} %param.14) | copy-start | bytes 73732
  10.9 0.7 %copy-start.2 = (s32[4,4,128]{2,1,0:T(4,128)S(1)}, s32[4,4,128]{2,1,0:T(4,128)}, u32[]{:S(2)}) copy-start(s32[4,4,128]{2,1,0:T(4,128)} %param.13) | copy-start | bytes 24580
  12.7 10.0 %collective-permute-start.2 = (bf16[6,1,64,128]{3,2,1,0:T(8,128)(2,1)S(1)}, bf16[6,1,64,128]{3,2,1,0:T(8,128)(2,1)S(1)}, u32[]{:S(2)}, u32[]{:S(2)}) collective-permute-start(bf16[6,1,64,128]{3,2,1,0:T(8,128)(2,1)S(1)} %pad_maximum_fusion), channel_id=1, source_target_pairs={{0,1},{1,2},{2,3},{3,4},{4,5},{5,6},{6,7},{7,8},{8,9},{9,10},{10,1... | collective-permute-start | bytes 294920 | tf_op jit(solution)/shard_map/ppermute | solution.py:27
  18.0 5.9 %collective-permute-start.3 = (bf16[6,1,64,128]{3,2,1,0:T(8,128)(2,1)S(1)}, bf16[6,1,64,128]{3,2,1,0:T(8,128)(2,1)S(1)}, u32[]{:S(2)}, u32[]{:S(2)}) collective-permute-start(bf16[6,1,64,128]{3,2,1,0:T(8,128)(2,1)S(1)} %pad_maximum_fusion.1), channel_id=1, source_target_pairs={{1,0},{2,1},{3,2},{4,3},{5,4},{6,5},{7,6},{8,7},{9,8},{10,9},{11,1... | collective-permute-start | bytes 294920 | tf_op jit(solution)/shard_map/ppermute | solution.py:27

commit v2 on v0

v2 whole, which is shorter than its diff:
```python
import jax
import jax.numpy as jnp
from jax import lax
from jax.experimental import pallas as pl
from jax.experimental.pallas import tpu as pltpu
from jax.sharding import PartitionSpec as P

BINS = 16
CORE = 4
TAPS = 3
FULL = (0, 1, 2)
VMEM_LIMIT = 32 * 1024 * 1024

VARIANTS = ((0, FULL), (1, FULL), (1, (0, 1)), (2, (1, 2)), (2, FULL), (3, FULL))
INNER = (1, 2, 3, 4)
OUTER = (0, 5)


def neighbours(axis, first, last):
    peers = lax.axis_size(axis)
    up = [(i, i + 1) for i in range(peers - 1)]
    down = [(j, i) for i, j in up]
    return lax.ppermute(last, axis, up), lax.ppermute(first, axis, down)


def variant_weights(axis):
    index, total = lax.axis_index(axis), lax.axis_size(axis)
    lower = jnp.where(index > 0, 1.0, 0.0)
    upper = jnp.where(index < total - 1, 1.0, 0.0)
    weights = (3.0 + 2.0 * lower, 4.0, lower, upper, 4.0, 3.0 + 2.0 * upper)
    cover = (3.0 + 2.0 * lower, 4.0 + lower, 4.0 + upper, 3.0 + 2.0 * upper)
    return weights, cover


def column_of(row, size):
    length = row.shape[1]
    down = lax.broadcasted_iota(jnp.int32, (size, length), 0)
    along = lax.broadcasted_iota(jnp.int32, (size, length), 1)
    return jnp.broadcast_to(jnp.sum(jnp.where(down == along, row, 0.0), axis=1, keepdims=True), (size, 128))


def arrange_kernel(f_ref, cells_ref, yfirst_ref, ylast_ref, zfirst_ref, zlast_ref, wide, f_v, sem):
    copy = pltpu.make_async_copy(f_ref, f_v, sem)
    copy.start()
    copy.wait()
    wide[...] = f_v[...].astype(jnp.float32)
    for y in range(CORE):
        for z in range(CORE):
            cell = wide[pl.ds(z * CORE + y, 64, stride=16), :].astype(jnp.bfloat16)
            cells_ref[y, z] = cell
            if y == 0:
                yfirst_ref[0, z] = cell
            if y == CORE - 1:
                ylast_ref[0, z] = cell
            if z == 0:
                zfirst_ref[y, 0] = cell
            if z == CORE - 1:
                zlast_ref[y, 0] = cell


def prepare_kernel(
    ids_hbm, bins_hbm, map_hbm, taps_hbm, cb_hbm, hb_hbm, hw_hbm,
    a_ref, col_ref, w_ref, bias_ref, off_ref, hw_ref,
    ids_ref, bins_ref, map_ref, taps_ref, cb_ref, hb_ref, row_ref, sems,
):
    pairs = (
        (ids_hbm, ids_ref), (map_hbm, map_ref), (bins_hbm, bins_ref), (taps_hbm, taps_ref), (cb_hbm, cb_ref),
        (hb_hbm, hb_ref), (hw_hbm, hw_ref),
    )
    copies = [pltpu.make_async_copy(src, dst, sems.at[i]) for i, (src, dst) in enumerate(pairs)]
    for copy in copies:
        copy.start()
    for copy in copies:
        copy.wait()
    one = jnp.ones((), jnp.bfloat16)
    none = jnp.zeros((), jnp.bfloat16)
    bins = bins_ref[...]
    for block in range(6):
        rows = slice(block * 8, block * 8 + 8)
        ids = ids_ref[rows]
        edge = jnp.maximum(ids, 0)
        low = edge & 127
        high = edge >> 7
        slot = jnp.zeros((8, 128), jnp.int32)
        for h in range(32):
            line = jnp.broadcast_to(map_ref[h : h + 1], (8, 128))
            slot = jnp.where(high == h, jnp.take_along_axis(line, low, axis=1, mode="promise_in_bounds"), slot)
        owner = slot >> 3
        first = block % 2 * 8
        column = (owner >> 8) * 128 + (slot & 7) * BINS + bins[first : first + 8]
        col_ref[rows] = jnp.where(ids >= 0, column, -1).astype(jnp.float32)
        row_ref[rows] = (owner & 255).astype(jnp.float32)
    count = lax.broadcasted_iota(jnp.int32, (256, 128), 0).astype(jnp.float32).astype(jnp.bfloat16)
    for r in range(48):
        row = row_ref[r : r + 1].astype(jnp.bfloat16)
        a_ref[:, r * 128 : r * 128 + 128] = jnp.where(count == row, one, none)
    for dx in range(TAPS):
        rows = jnp.concatenate([taps_ref[t % 3, t // 3, dx] for t in range(9)], axis=1)
        w_ref[64 * dx : 64 * dx + 64, :576] = rows
        w_ref[64 * dx : 64 * dx + 64, 640:1024] = rows[:, 192:]
    bias_ref[...] = column_of(cb_ref[...], 64)
    off_ref[...] = column_of(hb_ref[...], 8)


def predictions(zs, cell, w_ref, bias_ref, hw_ref, hb_ref, g_ref):
    width = 128 * len(zs)
    zero = jnp.zeros((64, 128), jnp.bfloat16)
    for y in range(6):
        for dz in range(TAPS):
            for i, v in enumerate(zs):
                z, kept = VARIANTS[v]
                part = cell(y, z + dz) if dz in kept else zero
                g_ref[(y * 3 + dz) * 64 : (y * 3 + dz) * 64 + 64, i * 128 : i * 128 + 128] = part
    lane = lax.broadcasted_iota(jnp.int32, (64, 128), 1)
    bias = bias_ref[...]
    preds = {}

    def matmul(left, right):
        return lax.dot_general(left, right, (((1,), (0,)), ((), ())), preferred_element_type=jnp.float32)

    def finish(yv, start, p):
        hidden = []
        for half in range(2):
            q = p[:, half * 128 : half * 128 + 128]
            before = jnp.where(lane == 0, 0.0, pltpu.roll(q[:64], 1, 1))
            after = jnp.where(lane == 127, 0.0, pltpu.roll(q[128:], 127, 1))
            pre = before + q[64:128] + after
            hidden.append(jnp.maximum(pre + bias, 0.0).astype(jnp.bfloat16))
        logits = matmul(hw_ref[...], jnp.concatenate(hidden, axis=1))
        for half in range(2):
            logit = logits[:, half * 128 : half * 128 + 128] + hb_ref[:3]
            preds[zs[start // 128 + half], yv] = jax.nn.sigmoid(logit)

    for start in range(0, width, 256):
        cols = slice(start, start + 256)
        finish(0, start, matmul(w_ref[:, :576], g_ref[:576, cols]))
        cut = matmul(w_ref[:, :384], g_ref[192:576, cols])
        finish(2, start, cut)
        finish(1, start, cut + matmul(w_ref[:, 832:1024], g_ref[576:768, cols]))
        cut = matmul(w_ref[:, 640:1024], g_ref[576:960, cols])
        finish(3, start, cut)
        finish(4, start, cut + matmul(w_ref[:, :192], g_ref[384:576, cols]))
        finish(5, start, matmul(w_ref[:, :576], g_ref[576:1152, cols]))
    return preds


def weighted(preds, totals):
    zweights, yweights = variant_weights("gz")[0], variant_weights("xy")[0]
    for (zv, yv), pred in preds.items():
        at = VARIANTS[zv][0] * CORE + VARIANTS[yv][0]
        term = pred * (zweights[zv] * yweights[yv])
        totals[at] = term if at not in totals else totals[at] + term
    return totals


def inner_kernel(f_ref, ylo_ref, yhi_ref, w_ref, bias_ref, hw_ref, hb_ref, sums_ref, g_ref):
    def cell(y, z):
        return ylo_ref[0, z - 1] if y == 0 else (yhi_ref[0, z - 1] if y == 5 else f_ref[y - 1, z - 1])

    preds = predictions(INNER, cell, w_ref, bias_ref, hw_ref, hb_ref, g_ref)
    for at, total in weighted(preds, {}).items():
        sums_ref[at, :3] = total


def outer_kernel(
    f_ref, ylo_ref, yhi_ref, zlo_ref, zhi_ref, w_ref, bias_ref, hw_ref, hb_ref, sums_ref, a_ref, col_ref,
    out_ref, table_ref, g_ref, b_ref,
):
    def cell(y, z):
        if z == 0 or z == 5:
            return (zlo_ref if z == 0 else zhi_ref)[y, 0]
        return ylo_ref[0, z - 1] if y == 0 else (yhi_ref[0, z - 1] if y == 5 else f_ref[y - 1, z - 1])

    preds = predictions(OUTER, cell, w_ref, bias_ref, hw_ref, hb_ref, g_ref)
    totals = weighted(preds, {at: sums_ref[at, :3] for at in range(16) if at // CORE in (1, 2)})
    zcover, ycover = variant_weights("gz")[1], variant_weights("xy")[1]
    for at in range(16):
        blend = totals[at] / (zcover[at // CORE] * ycover[at % CORE])
        for a in range(3):
            out_ref[a * 16 + at : a * 16 + at + 1, :] = blend[a : a + 1]
    count = lax.broadcasted_iota(jnp.int32, (256, 128), 0).astype(jnp.float32).astype(jnp.bfloat16)
    none = jnp.zeros((), jnp.bfloat16)
    for r in range(48):
        value = out_ref[r : r + 1].astype(jnp.bfloat16)
        here = count == col_ref[r : r + 1].astype(jnp.bfloat16)
        b_ref[:, r * 128 : r * 128 + 128] = jnp.where(here, value, none)
    both = lax.dot_general(
        a_ref[...], b_ref[...], (((1,), (1,)), ((), ())), preferred_element_type=jnp.float32
    )
    table_ref[:256] = both[:, :128].astype(jnp.bfloat16)
    table_ref[256:] = both[:, 128:].astype(jnp.bfloat16)


def vmem(count):
    return [pl.BlockSpec(memory_space=pltpu.VMEM)] * count


def shape(dims, dtype):
    return jax.ShapeDtypeStruct(dims, dtype)


def in_hbm(array):
    return pltpu.with_memory_space_constraint(array, pltpu.HBM)


def arrange(features):
    yface, zface = shape((1, CORE, 64, 128), jnp.bfloat16), shape((CORE, 1, 64, 128), jnp.bfloat16)
    return pl.pallas_call(
        arrange_kernel,
        out_shape=(shape((CORE, CORE, 64, 128), jnp.bfloat16), yface, yface, zface, zface),
        in_specs=[pl.BlockSpec(memory_space=pltpu.HBM)],
        out_specs=tuple(vmem(5)),
        scratch_shapes=[
            pltpu.VMEM((1024, 128), jnp.float32), pltpu.VMEM((1024, 128), jnp.bfloat16), pltpu.SemaphoreType.DMA(()),
        ],
        compiler_params=pltpu.CompilerParams(vmem_limit_bytes=VMEM_LIMIT),
        name="arrange",
    )(in_hbm(features))


def prepare(*operands):
    return pl.pallas_call(
        prepare_kernel,
        out_shape=(
            shape((256, 6144), jnp.bfloat16), shape((48, 128), jnp.float32), shape((192, 1024), jnp.bfloat16),
            shape((64, 128), jnp.float32), shape((8, 128), jnp.float32), shape((3, 64), jnp.bfloat16),
        ),
        in_specs=[pl.BlockSpec(memory_space=pltpu.HBM)] * 7,
        out_specs=tuple(vmem(6)),
        scratch_shapes=[pltpu.VMEM(o.shape, o.dtype) for o in operands[:-1]]
        + [pltpu.VMEM((48, 128), jnp.float32), pltpu.SemaphoreType.DMA((7,))],
        compiler_params=pltpu.CompilerParams(vmem_limit_bytes=VMEM_LIMIT),
        cost_estimate=pl.CostEstimate(flops=10**9, bytes_accessed=10**7, transcendentals=0),
        name="prepare",
    )(*map(in_hbm, operands))


def inner(*operands):
    return pl.pallas_call(
        inner_kernel,
        out_shape=shape((16, 8, 128), jnp.float32),
        in_specs=vmem(7),
        out_specs=vmem(1)[0],
        scratch_shapes=[pltpu.VMEM((6 * 192, 512), jnp.bfloat16)],
        compiler_params=pltpu.CompilerParams(vmem_limit_bytes=VMEM_LIMIT),
        cost_estimate=pl.CostEstimate(flops=2 * 10**9, bytes_accessed=10**6, transcendentals=0),
        name="inner",
    )(*operands)


def outer(*operands):
    return pl.pallas_call(
        outer_kernel,
        out_shape=(shape((48, 128), jnp.float32), shape((512, 128), jnp.bfloat16)),
        in_specs=vmem(12),
        out_specs=tuple(vmem(2)),
        scratch_shapes=[pltpu.VMEM((6 * 192, 256), jnp.bfloat16), pltpu.VMEM((256, 6144), jnp.bfloat16)],
        compiler_params=pltpu.CompilerParams(vmem_limit_bytes=VMEM_LIMIT),
        name="outer",
    )(*operands)


def on_device(features, conv_w, conv_b, head_w, head_b, bins, edge_ids, owner_map):
    gz_peers, xy_peers = lax.axis_size("gz"), lax.axis_size("xy")
    cells, yfirst, ylast, zfirst, zlast = arrange(features.reshape(1024, 128))
    ylo, yhi = neighbours("xy", yfirst, ylast)
    owners, columns, weights, bias, offset, heads = prepare(
        edge_ids.reshape(48, 128), bins.reshape(16, 128), owner_map.reshape(32, 128),
        jnp.transpose(conv_w, (2, 3, 4, 0, 1)), conv_b.reshape(1, 64), head_b.reshape(1, 3), head_w,
    )
    first = jnp.concatenate([ylo[:, :1], zfirst, yhi[:, :1]], axis=0)
    last = jnp.concatenate([ylo[:, CORE - 1 :], zlast, yhi[:, CORE - 1 :]], axis=0)
    zlo, zhi = neighbours("gz", first, last)
    sums = inner(cells, ylo, yhi, weights, bias, heads, offset)
    blended, table = outer(cells, ylo, yhi, zlo, zhi, weights, bias, heads, offset, sums, owners, columns)
    parts = lax.all_to_all(table.reshape(gz_peers, xy_peers, 128), "gz", 0, 0, tiled=True)
    sums = jnp.sum(parts.astype(jnp.float32), axis=0)
    share = jnp.sum(lax.all_to_all(sums, "xy", 0, 0, tiled=True), axis=0, keepdims=True)
    return blended.reshape(3, CORE, CORE, 128), share


def solution(mesh):
    in_specs = (
        P(None, "gz", "xy", None),
        P(),
        P(),
        P(),
        P(),
        P("gz", "xy", None),
        P(None, "gz", "xy", None),
        P(),
    )
    out_specs = (P(None, "gz", "xy", None), P(("gz", "xy"), None))
    return jax.shard_map(
        on_device, mesh=mesh, in_specs=in_specs, out_specs=out_specs, check_vma=False
    )
```

time: 423 us -> 63.8 us (0.15)
  waiting for transfers between devices: 287 us -> 1.55 us
  local copies, waits for them, and re-layouts: 40.5 us -> 0.01 us
  other arithmetic: 39.1 us -> 0.61 us
  blocking collectives: 0 us -> 38.1 us
  matrix products: 17.5 us -> 0 us
  between operations: 14.4 us -> 0.74 us
  starting transfers between devices: 23.3 us -> 13.3 us
  Pallas kernels: 0 us -> 9.16 us
    unnamed x2 -> x0, waiting for transfers between devices: 273 us -> none
    all_to_all x0 -> x2, blocking collectives: none -> 38.1 us  [the longest x1 19.7 us: on_device(): lax.all_to_all(table.reshape(gz_peers, xy_peers, 128), 'gz', 0, 0, tiled=...]
    gather x1 -> x0, local copies, waits for them, and re-layouts: 34.3 us -> none  [on_device(): slots = owner_map[jnp.maximum(edge_ids, 0)]]
    scatter-add x5 -> x0, other arithmetic: 33.3 us -> none  [the longest x1 33.2 us: on_device(): jax.ops.segment_sum(values.reshape(-1), index.reshape(-1), num_segments=e...]
    conv_general_dilated x1 -> x0, matrix products: 16.9 us -> none  [convolve(): lax.conv_general_dilated(source[None], weights, (1, 1, 1), spacing, dimen...]
    ppermute x8 -> x4, waiting for transfers between devices: 14.2 us -> 1.55 us  [neighbours(): return (lax.ppermute(last, axis, up), lax.ppermute(first, axis, down))]
    ppermute x8 -> x4, starting transfers between devices: 23.3 us -> 13.3 us  [neighbours(): return (lax.ppermute(last, axis, up), lax.ppermute(first, axis, down))]
    pallas_call x0 -> x4, Pallas kernels: none -> 9.16 us  [the longest x1 3.1 us: outer(): pl.pallas_call(outer_kernel, out_shape=(shape((48, 128), jnp.float32), sh...]
  transfers between devices with their start and end apart: 9 -> 4, of which waited for: 5 -> 1; matrix products, arithmetic and copies ran while one was open for 8% -> 0% of each run, Pallas kernels for 0% -> 8%
where the time goes in v2:
time: 63.8 us; the launch traced here: 63.5 us
  blocking collectives  38.1 us (60%)
  starting transfers between devices  13.3 us (21%)
  Pallas kernels  9.16 us (14%)
  waiting for transfers between devices  1.55 us (2%)
  between operations  0.74 us (1%)
    all_to_all x1, blocking collectives, on_device(): lax.all_to_all(table.reshape(gz_peers, xy_peers, 128), 'gz', 0, 0, tiled=...  19.7 us
    all_to_all x1, blocking collectives, on_device(): lax.all_to_all(sums, 'xy', 0, 0, tiled=True)  18.5 us
    ppermute x4, starting transfers between devices, neighbours(): return (lax.ppermute(last, axis, up), lax.ppermute(first, axis, down))  13.3 us
    pallas_call x1, Pallas kernels, outer(): pl.pallas_call(outer_kernel, out_shape=(shape((48, 128), jnp.float32), sh...  3.1 us
    pallas_call x1, Pallas kernels, inner(): pl.pallas_call(inner_kernel, out_shape=shape((16, 8, 128), jnp.float32),...  2.78 us
    pallas_call x1, Pallas kernels, prepare(): pl.pallas_call(prepare_kernel, out_shape=(shape((256, 6144), jnp.bfloat16...  2.13 us
    ppermute x4, waiting for transfers between devices, neighbours(): return (lax.ppermute(last, axis, up), lax.ppermute(first, axis, down))  1.55 us
  transfers between devices with their start and end apart: 4, of which 1 were waited for; matrix products, arithmetic and copies ran while one was open for 0% of the time, Pallas kernels for 8%

profile of v2, /device:TPU:1, one launch (start us, length us, event | category | flops | bytes accessed | tf_op | source)
XLA Modules:
  0.0 63.5 jit_solution(6252466364234126912)
XLA Ops:
  0.6 1.2 %arrange.1 = (bf16[4,4,64,128]{3,2,1,0:T(8,128)(2,1)S(1)}, bf16[1,4,64,128]{3,2,1,0:T(8,128)(2,1)S(1)}, bf16[1,4,64,128]{3,2,1,0:T(8,128)(2,1)S(1)}, bf16[4,1,64...) custom-call(bf16[1024,128]{1,0:T(8,128)(2,1)} %bitcast.12), custom_call_target="tpu_custom_call" | custom-call | tf_op jit(solution)/shard_map/arrange/pallas_call | solution.py:208
  1.8 5.4 %collective-permute-start = (bf16[1,4,64,128]{3,2,1,0:T(8,128)(2,1)S(1)}, bf16[1,4,64,128]{3,2,1,0:T(8,128)(2,1)S(1)}, u32[]{:S(2)}, u32[]{:S(2)}) collective-permute-start(bf16[1,4,64,128]{3,2,1,0:T(8,128)(2,1)S(1)} %get-tuple-element.16), channel_id=1, source_target_pairs={{0,1},{1,2},{2,3},{3,4},{4,5},{5,6},{6,7},{7,8},{8,9},{9,10},{10,1... | collective-permute-start | bytes 196616 | tf_op jit(solution)/shard_map/ppermute | solution.py:23
  7.2 4.7 %collective-permute-start.1 = (bf16[1,4,64,128]{3,2,1,0:T(8,128)(2,1)S(1)}, bf16[1,4,64,128]{3,2,1,0:T(8,128)(2,1)S(1)}, u32[]{:S(2)}, u32[]{:S(2)}) collective-permute-start(bf16[1,4,64,128]{3,2,1,0:T(8,128)(2,1)S(1)} %get-tuple-element.17), channel_id=1, source_target_pairs={{1,0},{2,1},{3,2},{4,3},{5,4},{6,5},{7,6},{8,7},{9,8},{10,9},{11,1... | collective-permute-start | bytes 196616 | tf_op jit(solution)/shard_map/ppermute | solution.py:23
  11.9 2.1 %prepare.1 = (bf16[256,6144]{1,0:T(8,128)(2,1)S(1)}, f32[48,128]{1,0:T(8,128)S(1)}, bf16[192,1024]{1,0:T(8,128)(2,1)S(1)}, f32[64,128]{1,0:T(8,128)S(1)}, f32[8,...) custom-call(s32[48,128]{1,0:T(8,128)} %bitcast.16, s32[16,128]{1,0:T(8,128)} %bitcast.19, s32[32,128]{1,0:T(8,128)} %bitcast.18, ...), custom_call_target="tpu_custom_call" | custom-call | flops 1000000000 | bytes 10000000 | tf_op jit(solution)/shard_map/prepare/pallas_call | solution.py:222
  14.0 0.0 collective-permute-done.ylo_ref
  14.0 0.0 collective-permute-done.1.yhi_ref
  14.1 1.9 %collective-permute-start.2 = (bf16[6,1,64,128]{3,2,1,0:T(8,128)(2,1)S(1)}, bf16[6,1,64,128]{3,2,1,0:T(8,128)(2,1)S(1)}, u32[]{:S(2)}, u32[]{:S(2)}) collective-permute-start(bf16[6,1,64,128]{3,2,1,0:T(8,128)(2,1)S(1)} %pad_maximum_fusion), channel_id=1, source_target_pairs={{0,16},{16,32},{32,48},{48,64},{64,80},{80,96},{96,112},{112,128},... | collective-permute-start | bytes 294920 | tf_op jit(solution)/shard_map/ppermute | solution.py:23
  16.0 1.3 %collective-permute-start.3 = (bf16[6,1,64,128]{3,2,1,0:T(8,128)(2,1)S(1)}, bf16[6,1,64,128]{3,2,1,0:T(8,128)(2,1)S(1)}, u32[]{:S(2)}, u32[]{:S(2)}) collective-permute-start(bf16[6,1,64,128]{3,2,1,0:T(8,128)(2,1)S(1)} %pad_maximum_fusion.1), channel_id=1, source_target_pairs={{16,0},{32,16},{48,32},{64,48},{80,64},{96,80},{112,96},{128,112},... | collective-permute-start | bytes 294920 | tf_op jit(solution)/shard_map/ppermute | solution.py:23
  17.3 2.8 %inner.1.sums_ref = f32[16,8,128]{2,1,0:T(8,128)S(1)} custom-call(bf16[4,4,64,128]{3,2,1,0:T(8,128)(2,1)S(1)} %get-tuple-element.15.f_ref, bf16[1,4,64,128]{3,2,1,0:T(8,128)(2,1)S(1)} %collective-permute-done.ylo_ref, bf16[1,4,64,128]{3,2,1,0:T(8,128)(2,1)S(1)} %collective-permute-done.1.yhi_ref, bf16[192,1024]{1,0:T(8,128)(2,1)S(1)} %get-tuple-element.20.w_ref, ...), custom_call_target="tpu_custom_call" | custom-call | flops 2000000000 | bytes 1000000 | tf_op jit(solution)/shard_map/inner/pallas_call | solution.py:239
  20.1 0.0 collective-permute-done.2.zlo_ref
  20.1 1.5 %collective-permute-done.3.zhi_ref = bf16[6,1,64,128]{3,2,1,0:T(8,128)(2,1)S(1)} collective-permute-done((bf16[6,1,64,128]{3,2,1,0:T(8,128)(2,1)S(1)}, bf16[6,1,64,128]{3,2,1,0:T(8,128)(2,1)S(1)}, u32[]{:S(2)}, u32[]{:S(2)}) %collective-permute-start.3) | collective-permute-done | bytes 98336 | tf_op jit(solution)/shard_map/ppermute | solution.py:23
  21.7 3.1 %outer.1 = (f32[48,128]{1,0:T(8,128)}, bf16[512,128]{1,0:T(8,128)(2,1)S(1)}) custom-call(bf16[4,4,64,128]{3,2,1,0:T(8,128)(2,1)S(1)} %get-tuple-element.15.f_ref, bf16[1,4,64,128]{3,2,1,0:T(8,128)(2,1)S(1)} %collective-permute-done.ylo_ref, bf16[1,4,64,128]{3,2,1,0:T(8,128)(2,1)S(1)} %collective-permute-done.1.yhi_ref, ...), custom_call_target="tpu_custom_call" | custom-call | tf_op jit(solution)/shard_map/outer/pallas_call | solution.py:252
  24.8 19.7 %all_to_all.14 = bf16[32,16,128]{2,1,0:T(8,128)(2,1)S(1)} all-to-all(bf16[32,16,128]{2,1,0:T(8,128)(2,1)S(1)} %bitcast.11), channel_id=1, replica_groups=mesh['gz'=32,'xy'=16] {'gz'}, dimensions={0} | all-to-all | bytes 262144 | tf_op jit(solution)/shard_map/all_to_all | solution.py:276
  44.5 18.5 %all_to_all.15 = f32[16,1,128]{2,1,0:T(1,128)S(1)} all-to-all(f32[16,1,128]{2,1,0:T(1,128)S(1)} %bitcast.13), channel_id=1, replica_groups=mesh['gz'=32,'xy'=16] {'xy'}, dimensions={0} | all-to-all | bytes 16384 | tf_op jit(solution)/shard_map/all_to_all | solution.py:278
  63.0 0.5 reduce_sum.19
  (5 shorter events, 0.1 us)
Async XLA Ops:
  1.8 12.2 %collective-permute-start = (bf16[1,4,64,128]{3,2,1,0:T(8,128)(2,1)S(1)}, bf16[1,4,64,128]{3,2,1,0:T(8,128)(2,1)S(1)}, u32[]{:S(2)}, u32[]{:S(2)}) collective-permute-start(bf16[1,4,64,128]{3,2,1,0:T(8,128)(2,1)S(1)} %get-tuple-element.16), channel_id=1, source_target_pairs={{0,1},{1,2},{2,3},{3,4},{4,5},{5,6},{6,7},{7,8},{8,9},{9,10},{10,1... | collective-permute-start | bytes 196616 | tf_op jit(solution)/shard_map/ppermute | solution.py:23
  7.2 6.9 %collective-permute-start.1 = (bf16[1,4,64,128]{3,2,1,0:T(8,128)(2,1)S(1)}, bf16[1,4,64,128]{3,2,1,0:T(8,128)(2,1)S(1)}, u32[]{:S(2)}, u32[]{:S(2)}) collective-permute-start(bf16[1,4,64,128]{3,2,1,0:T(8,128)(2,1)S(1)} %get-tuple-element.17), channel_id=1, source_target_pairs={{1,0},{2,1},{3,2},{4,3},{5,4},{6,5},{7,6},{8,7},{9,8},{10,9},{11,1... | collective-permute-start | bytes 196616 | tf_op jit(solution)/shard_map/ppermute | solution.py:23
  14.1 6.0 %collective-permute-start.2 = (bf16[6,1,64,128]{3,2,1,0:T(8,128)(2,1)S(1)}, bf16[6,1,64,128]{3,2,1,0:T(8,128)(2,1)S(1)}, u32[]{:S(2)}, u32[]{:S(2)}) collective-permute-start(bf16[6,1,64,128]{3,2,1,0:T(8,128)(2,1)S(1)} %pad_maximum_fusion), channel_id=1, source_target_pairs={{0,16},{16,32},{32,48},{48,64},{64,80},{80,96},{96,112},{112,128},... | collective-permute-start | bytes 294920 | tf_op jit(solution)/shard_map/ppermute | solution.py:23
  16.0 5.6 %collective-permute-start.3 = (bf16[6,1,64,128]{3,2,1,0:T(8,128)(2,1)S(1)}, bf16[6,1,64,128]{3,2,1,0:T(8,128)(2,1)S(1)}, u32[]{:S(2)}, u32[]{:S(2)}) collective-permute-start(bf16[6,1,64,128]{3,2,1,0:T(8,128)(2,1)S(1)} %pad_maximum_fusion.1), channel_id=1, source_target_pairs={{16,0},{32,16},{48,32},{64,48},{80,64},{96,80},{112,96},{128,112},... | collective-permute-start | bytes 294920 | tf_op jit(solution)/shard_map/ppermute | solution.py:23

commit v3 on v2

--- a/solution.py
+++ b/solution.py
@@ -1,5 +1,6 @@
 import jax
 import jax.numpy as jnp
+import numpy as np
 from jax import lax
 from jax.experimental import pallas as pl
 from jax.experimental.pallas import tpu as pltpu
@@ -14,13 +15,19 @@
 VARIANTS = ((0, FULL), (1, FULL), (1, (0, 1)), (2, (1, 2)), (2, FULL), (3, FULL))
 INNER = (1, 2, 3, 4)
 OUTER = (0, 5)
-
-
-def neighbours(axis, first, last):
+INNER_ROWS = [(axis, at) for axis in range(3) for at in range(4, 12)]
+OUTER_ROWS = [(axis, at) for axis in range(3) for at in (0, 1, 2, 3, 12, 13, 14, 15)]
+
+
+def swaps(axis, inside, outside):
     peers = lax.axis_size(axis)
-    up = [(i, i + 1) for i in range(peers - 1)]
-    down = [(j, i) for i, j in up]
-    return lax.ppermute(last, axis, up), lax.ppermute(first, axis, down)
+    near = [(i, i ^ 1) for i in range(peers)]
+    far = [(i, ((i + 1) ^ 1) - 1) for i in range(1, peers - 1)]
+    return lax.ppermute(inside, axis, near), lax.ppermute(outside, axis, far)
+
+
+def is_even(axis):
+    return lax.axis_index(axis) % 2 == 0
 
 
 def variant_weights(axis):
@@ -39,23 +46,25 @@
     return jnp.broadcast_to(jnp.sum(jnp.where(down == along, row, 0.0), axis=1, keepdims=True), (size, 128))
 
 
-def arrange_kernel(f_ref, cells_ref, yfirst_ref, ylast_ref, zfirst_ref, zlast_ref, wide, f_v, sem):
+def arrange_kernel(f_ref, cells_ref, ynear_ref, yfar_ref, znear_ref, zfar_ref, wide, f_v, sem):
     copy = pltpu.make_async_copy(f_ref, f_v, sem)
     copy.start()
     copy.wait()
     wide[...] = f_v[...].astype(jnp.float32)
+    cells = {}
     for y in range(CORE):
         for z in range(CORE):
-            cell = wide[pl.ds(z * CORE + y, 64, stride=16), :].astype(jnp.bfloat16)
-            cells_ref[y, z] = cell
-            if y == 0:
-                yfirst_ref[0, z] = cell
-            if y == CORE - 1:
-                ylast_ref[0, z] = cell
-            if z == 0:
-                zfirst_ref[y, 0] = cell
-            if z == CORE - 1:
-                zlast_ref[y, 0] = cell
+            cells[y, z] = wide[pl.ds(z * CORE + y, 64, stride=16), :].astype(jnp.bfloat16)
+            cells_ref[y, z] = cells[y, z]
+    last = CORE - 1
+    even = is_even("xy")
+    for z in range(CORE):
+        ynear_ref[0, z] = jnp.where(even, cells[last, z], cells[0, z])
+        yfar_ref[0, z] = jnp.where(even, cells[0, z], cells[last, z])
+    even = is_even("gz")
+    for y in range(CORE):
+        znear_ref[y, 0] = jnp.where(even, cells[y, last], cells[y, 0])
+        zfar_ref[y, 0] = jnp.where(even, cells[y, 0], cells[y, last])
 
 
 def prepare_kernel(
@@ -86,14 +95,16 @@
             line = jnp.broadcast_to(map_ref[h : h + 1], (8, 128))
             slot = jnp.where(high == h, jnp.take_along_axis(line, low, axis=1, mode="promise_in_bounds"), slot)
         owner = slot >> 3
+        place = (owner & 384) + ((owner & 1) << 6) + ((owner >> 1) & 63)
         first = block % 2 * 8
-        column = (owner >> 8) * 128 + (slot & 7) * BINS + bins[first : first + 8]
+        column = (place >> 8) * 128 + (slot & 7) * BINS + bins[first : first + 8]
         col_ref[rows] = jnp.where(ids >= 0, column, -1).astype(jnp.float32)
-        row_ref[rows] = (owner & 255).astype(jnp.float32)
+        row_ref[rows] = (place & 255).astype(jnp.float32)
     count = lax.broadcasted_iota(jnp.int32, (256, 128), 0).astype(jnp.float32).astype(jnp.bfloat16)
-    for r in range(48):
+    for i, (axis, at) in enumerate(INNER_ROWS + OUTER_ROWS):
+        r = axis * 16 + at
         row = row_ref[r : r + 1].astype(jnp.bfloat16)
-        a_ref[:, r * 128 : r * 128 + 128] = jnp.where(count == row, one, none)
+        a_ref[:, i * 128 : i * 128 + 128] = jnp.where(count == row, one, none)
     for dx in range(TAPS):
         rows = jnp.concatenate([taps_ref[t % 3, t // 3, dx] for t in range(9)], axis=1)
         w_ref[64 * dx : 64 * dx + 64, :576] = rows
@@ -144,49 +155,73 @@
     return preds
 
 
-def weighted(preds, totals):
-    zweights, yweights = variant_weights("gz")[0], variant_weights("xy")[0]
+def blend(preds):
+    zweights, zcover = variant_weights("gz")
+    yweights, ycover = variant_weights("xy")
+    totals = {}
     for (zv, yv), pred in preds.items():
         at = VARIANTS[zv][0] * CORE + VARIANTS[yv][0]
         term = pred * (zweights[zv] * yweights[yv])
         totals[at] = term if at not in totals else totals[at] + term
-    return totals
-
-
-def inner_kernel(f_ref, ylo_ref, yhi_ref, w_ref, bias_ref, hw_ref, hb_ref, sums_ref, g_ref):
+    return {at: total / (zcover[at // CORE] * ycover[at % CORE]) for at, total in totals.items()}
+
+
+def histogram(rows, value_ref, col_ref, a_ref, b_ref):
+    count = lax.broadcasted_iota(jnp.int32, (256, 128), 0).astype(jnp.float32).astype(jnp.bfloat16)
+    none = jnp.zeros((), jnp.bfloat16)
+    for i, (axis, at) in enumerate(rows):
+        r = axis * 16 + at
+        here = count == col_ref[r : r + 1].astype(jnp.bfloat16)
+        b_ref[:, i * 128 : i * 128 + 128] = jnp.where(here, value_ref[i : i + 1].astype(jnp.bfloat16), none)
+    return lax.dot_general(a_ref, b_ref[...], (((1,), (1,)), ((), ())), preferred_element_type=jnp.float32)
+
+
+def edges(near_ref, far_ref, axis):
+    even = is_even(axis)
+
+    def low(*at):
+        return jnp.where(even, far_ref[at], near_ref[at])
+
+    def high(*at):
+        return jnp.where(even, near_ref[at], far_ref[at])
+
+    return low, high
+
+
+def inner_kernel(
+    f_ref, ynear_ref, yfar_ref, w_ref, bias_ref, hw_ref, hb_ref, a_ref, col_ref, part_ref, counts_ref, g_ref, b_ref
+):
+    ylow, yhigh = edges(ynear_ref, yfar_ref, "xy")
+
     def cell(y, z):
-        return ylo_ref[0, z - 1] if y == 0 else (yhi_ref[0, z - 1] if y == 5 else f_ref[y - 1, z - 1])
-
-    preds = predictions(INNER, cell, w_ref, bias_ref, hw_ref, hb_ref, g_ref)
-    for at, total in weighted(preds, {}).items():
-        sums_ref[at, :3] = total
+        return ylow(0, z - 1) if y == 0 else (yhigh(0, z - 1) if y == 5 else f_ref[y - 1, z - 1])
+
+    blends = blend(predictions(INNER, cell, w_ref, bias_ref, hw_ref, hb_ref, g_ref))
+    for i, (axis, at) in enumerate(INNER_ROWS):
+        part_ref[i : i + 1] = blends[at][axis : axis + 1]
+    counts_ref[...] = histogram(INNER_ROWS, part_ref, col_ref, a_ref[:, : 24 * 128], b_ref)
 
 
 def outer_kernel(
-    f_ref, ylo_ref, yhi_ref, zlo_ref, zhi_ref, w_ref, bias_ref, hw_ref, hb_ref, sums_ref, a_ref, col_ref,
-    out_ref, table_ref, g_ref, b_ref,
+    f_ref, ynear_ref, yfar_ref, znear_ref, zfar_ref, w_ref, bias_ref, hw_ref, hb_ref, a_ref, col_ref, part_ref, counts_ref,
+    out_ref, table_ref, g_ref, b_ref, value_ref,
 ):
+    ylow, yhigh = edges(ynear_ref, yfar_ref, "xy")
+    zlow, zhigh = edges(znear_ref, zfar_ref, "gz")
+
     def cell(y, z):
         if z == 0 or z == 5:
-            return (zlo_ref if z == 0 else zhi_ref)[y, 0]
-        return ylo_ref[0, z - 1] if y == 0 else (yhi_ref[0, z - 1] if y == 5 else f_ref[y - 1, z - 1])
-
-    preds = predictions(OUTER, cell, w_ref, bias_ref, hw_ref, hb_ref, g_ref)
-    totals = weighted(preds, {at: sums_ref[at, :3] for at in range(16) if at // CORE in (1, 2)})
-    zcover, ycover = variant_weights("gz")[1], variant_weights("xy")[1]
-    for at in range(16):
-        blend = totals[at] / (zcover[at // CORE] * ycover[at % CORE])
-        for a in range(3):
-            out_ref[a * 16 + at : a * 16 + at + 1, :] = blend[a : a + 1]
-    count = lax.broadcasted_iota(jnp.int32, (256, 128), 0).astype(jnp.float32).astype(jnp.bfloat16)
-    none = jnp.zeros((), jnp.bfloat16)
-    for r in range(48):
-        value = out_ref[r : r + 1].astype(jnp.bfloat16)
-        here = count == col_ref[r : r + 1].astype(jnp.bfloat16)
-        b_ref[:, r * 128 : r * 128 + 128] = jnp.where(here, value, none)
-    both = lax.dot_general(
-        a_ref[...], b_ref[...], (((1,), (1,)), ((), ())), preferred_element_type=jnp.float32
-    )
+            return (zlow if z == 0 else zhigh)(y, 0)
+        return ylow(0, z - 1) if y == 0 else (yhigh(0, z - 1) if y == 5 else f_ref[y - 1, z - 1])
+
+    blends = blend(predictions(OUTER, cell, w_ref, bias_ref, hw_ref, hb_ref, g_ref))
+    for i, (axis, at) in enumerate(OUTER_ROWS):
+        value_ref[i : i + 1] = blends[at][axis : axis + 1]
+    for axis in range(3):
+        out_ref[axis * 16 : axis * 16 + 4] = value_ref[axis * 8 : axis * 8 + 4]
+        out_ref[axis * 16 + 4 : axis * 16 + 12] = part_ref[axis * 8 : axis * 8 + 8]
+        out_ref[axis * 16 + 12 : axis * 16 + 16] = value_ref[axis * 8 + 4 : axis * 8 + 8]
+    both = counts_ref[...] + histogram(OUTER_ROWS, value_ref, col_ref, a_ref[:, 24 * 128 :], b_ref)
     table_ref[:256] = both[:, :128].astype(jnp.bfloat16)
     table_ref[256:] = both[:, 128:].astype(jnp.bfloat16)
 
@@ -238,10 +273,10 @@
 def inner(*operands):
     return pl.pallas_call(
         inner_kernel,
-        out_shape=shape((16, 8, 128), jnp.float32),
-        in_specs=vmem(7),
-        out_specs=vmem(1)[0],
-        scratch_shapes=[pltpu.VMEM((6 * 192, 512), jnp.bfloat16)],
+        out_shape=(shape((24, 128), jnp.float32), shape((256, 256), jnp.float32)),
+        in_specs=vmem(9),
+        out_specs=tuple(vmem(2)),
+        scratch_shapes=[pltpu.VMEM((6 * 192, 512), jnp.bfloat16), pltpu.VMEM((256, 3072), jnp.bfloat16)],
         compiler_params=pltpu.CompilerParams(vmem_limit_bytes=VMEM_LIMIT),
         cost_estimate=pl.CostEstimate(flops=2 * 10**9, bytes_accessed=10**6, transcendentals=0),
         name="inner",
@@ -252,30 +287,48 @@
     return pl.pallas_call(
         outer_kernel,
         out_shape=(shape((48, 128), jnp.float32), shape((512, 128), jnp.bfloat16)),
-        in_specs=vmem(12),
+        in_specs=vmem(13),
         out_specs=tuple(vmem(2)),
-        scratch_shapes=[pltpu.VMEM((6 * 192, 256), jnp.bfloat16), pltpu.VMEM((256, 6144), jnp.bfloat16)],
+        scratch_shapes=[
+            pltpu.VMEM((6 * 192, 256), jnp.bfloat16), pltpu.VMEM((256, 3072), jnp.bfloat16),
+            pltpu.VMEM((24, 128), jnp.float32),
+        ],
         compiler_params=pltpu.CompilerParams(vmem_limit_bytes=VMEM_LIMIT),
         name="outer",
     )(*operands)
 
 
+def groups(kept):
+    ids = np.arange(512).reshape(4, 8, 8, 2)
+    return ids.transpose(1, 2, 0, 3).reshape(64, 8).tolist() if kept == "xc" else ids.transpose(0, 3, 1, 2).reshape(8, 64).tolist()
+
+
 def on_device(features, conv_w, conv_b, head_w, head_b, bins, edge_ids, owner_map):
-    gz_peers, xy_peers = lax.axis_size("gz"), lax.axis_size("xy")
-    cells, yfirst, ylast, zfirst, zlast = arrange(features.reshape(1024, 128))
-    ylo, yhi = neighbours("xy", yfirst, ylast)
+    last = CORE - 1
+    cells, ynear, yfar, znear, zfar = arrange(features.reshape(1024, 128))
+    ynear, yfar = swaps("xy", ynear, yfar)
     owners, columns, weights, bias, offset, heads = prepare(
         edge_ids.reshape(48, 128), bins.reshape(16, 128), owner_map.reshape(32, 128),
         jnp.transpose(conv_w, (2, 3, 4, 0, 1)), conv_b.reshape(1, 64), head_b.reshape(1, 3), head_w,
     )
-    first = jnp.concatenate([ylo[:, :1], zfirst, yhi[:, :1]], axis=0)
-    last = jnp.concatenate([ylo[:, CORE - 1 :], zlast, yhi[:, CORE - 1 :]], axis=0)
-    zlo, zhi = neighbours("gz", first, last)
-    sums = inner(cells, ylo, yhi, weights, bias, heads, offset)
-    blended, table = outer(cells, ylo, yhi, zlo, zhi, weights, bias, heads, offset, sums, owners, columns)
-    parts = lax.all_to_all(table.reshape(gz_peers, xy_peers, 128), "gz", 0, 0, tiled=True)
+    yeven, zeven = is_even("xy"), is_even("gz")
+    ylow, yhigh = jnp.where(yeven, yfar, ynear), jnp.where(yeven, ynear, yfar)
+
+    def with_corners(face, even):
+        low = jnp.where(even, ylow[:, last:], ylow[:, :1])
+        high = jnp.where(even, yhigh[:, last:], yhigh[:, :1])
+        return jnp.concatenate([low, face, high], axis=0)
+
+    znear, zfar = swaps("gz", with_corners(znear, zeven), with_corners(zfar, jnp.logical_not(zeven)))
+    part, counts = inner(cells, ynear, yfar, weights, bias, heads, offset, owners, columns)
+    blended, table = outer(
+        cells, ynear, yfar, znear, zfar, weights, bias, heads, offset, owners, columns, part, counts
+    )
+    every = ("gz", "xy")
+    parts = lax.all_to_all(table.reshape(8, 64, 128), every, 0, 0, tiled=True, axis_index_groups=groups("xc"))
     sums = jnp.sum(parts.astype(jnp.float32), axis=0)
-    share = jnp.sum(lax.all_to_all(sums, "xy", 0, 0, tiled=True), axis=0, keepdims=True)
+    sums = lax.all_to_all(sums, every, 0, 0, tiled=True, axis_index_groups=groups("yz"))
+    share = jnp.sum(sums, axis=0, keepdims=True)
     return blended.reshape(3, CORE, CORE, 128), share
 
 

time: 63.8 us -> 62.4 us (0.978)
  blocking collectives: 38.1 us -> 36.3 us
    all_to_all x2, blocking collectives: 38.1 us -> 36.3 us  [the longest x1 26.2 us: on_device(): lax.all_to_all(sums, every, 0, 0, tiled=True, axis_index_groups=groups('y...]
    pallas_call x1, Pallas kernels: 2.78 us -> 3.54 us  [inner(): pl.pallas_call(inner_kernel, out_shape=(shape((24, 128), jnp.float32), sh...]
  transfers between devices with their start and end apart: 4 -> 4, of which waited for: 1 -> 1; matrix products, arithmetic and copies ran while one was open for 0% -> 0% of each run, Pallas kernels for 8% -> 9%
where the time goes in v3:
time: 62.4 us; the launch traced here: 62.1 us
  blocking collectives  36.3 us (58%)
  starting transfers between devices  13.3 us (21%)
  Pallas kernels  9.62 us (15%)
  waiting for transfers between devices  1.49 us (2%)
  between operations  0.76 us (1%)
  other arithmetic  0.67 us (1%)
    all_to_all x1, blocking collectives, on_device(): lax.all_to_all(sums, every, 0, 0, tiled=True, axis_index_groups=groups('y...  26.2 us
    ppermute x4, starting transfers between devices, swaps(): return (lax.ppermute(inside, axis, near), lax.ppermute(outside, axis, far))  13.3 us
    all_to_all x1, blocking collectives, on_device(): lax.all_to_all(table.reshape(8, 64, 128), every, 0, 0, tiled=True, axis_i...  10.1 us
    pallas_call x1, Pallas kernels, inner(): pl.pallas_call(inner_kernel, out_shape=(shape((24, 128), jnp.float32), sh...  3.54 us
    pallas_call x1, Pallas kernels, outer(): pl.pallas_call(outer_kernel, out_shape=(shape((48, 128), jnp.float32), sh...  2.77 us
    pallas_call x1, Pallas kernels, prepare(): pl.pallas_call(prepare_kernel, out_shape=(shape((256, 6144), jnp.bfloat16...  2.13 us
    ppermute x4, waiting for transfers between devices, swaps(): return (lax.ppermute(inside, axis, near), lax.ppermute(outside, axis, far))  1.49 us
  transfers between devices with their start and end apart: 4, of which 1 were waited for; matrix products, arithmetic and copies ran while one was open for 0% of the time, Pallas kernels for 9%

profile of v3, /device:TPU:1, one launch (start us, length us, event | category | flops | bytes accessed | tf_op | source)
XLA Modules:
  0.0 62.1 jit_solution(12994341184101412108)
XLA Ops:
  0.6 1.2 %arrange.1 = (bf16[4,4,64,128]{3,2,1,0:T(8,128)(2,1)S(1)}, bf16[1,4,64,128]{3,2,1,0:T(8,128)(2,1)S(1)}, bf16[1,4,64,128]{3,2,1,0:T(8,128)(2,1)S(1)}, bf16[4,1,64...) custom-call(bf16[1024,128]{1,0:T(8,128)(2,1)} %bitcast.12), custom_call_target="tpu_custom_call" | custom-call | tf_op jit(solution)/shard_map/arrange/pallas_call | solution.py:243
  1.8 8.8 %collective-permute-start = (bf16[1,4,64,128]{3,2,1,0:T(8,128)(2,1)S(1)}, bf16[1,4,64,128]{3,2,1,0:T(8,128)(2,1)S(1)}, u32[]{:S(2)}, u32[]{:S(2)}) collective-permute-start(bf16[1,4,64,128]{3,2,1,0:T(8,128)(2,1)S(1)} %get-tuple-element.18), channel_id=1, source_target_pairs={{0,1},{1,0},{2,3},{3,2},{4,5},{5,4},{6,7},{7,6},{8,9},{9,8},{10,11... | collective-permute-start | bytes 196616 | tf_op jit(solution)/shard_map/ppermute | solution.py:26
  10.6 1.9 %collective-permute-start.1 = (bf16[1,4,64,128]{3,2,1,0:T(8,128)(2,1)S(1)}, bf16[1,4,64,128]{3,2,1,0:T(8,128)(2,1)S(1)}, u32[]{:S(2)}, u32[]{:S(2)}) collective-permute-start(bf16[1,4,64,128]{3,2,1,0:T(8,128)(2,1)S(1)} %get-tuple-element.19), channel_id=1, source_target_pairs={{1,2},{2,1},{3,4},{4,3},{5,6},{6,5},{7,8},{8,7},{9,10},{10,9},{11,... | collective-permute-start | bytes 196616 | tf_op jit(solution)/shard_map/ppermute | solution.py:26
  12.6 2.1 %prepare.1 = (bf16[256,6144]{1,0:T(8,128)(2,1)S(1)}, f32[48,128]{1,0:T(8,128)S(1)}, bf16[192,1024]{1,0:T(8,128)(2,1)S(1)}, f32[64,128]{1,0:T(8,128)S(1)}, f32[8,...) custom-call(s32[48,128]{1,0:T(8,128)} %bitcast.16, s32[16,128]{1,0:T(8,128)} %bitcast.19, s32[32,128]{1,0:T(8,128)} %bitcast.18, ...), custom_call_target="tpu_custom_call" | custom-call | flops 1000000000 | bytes 10000000 | tf_op jit(solution)/shard_map/prepare/pallas_call | solution.py:257
  14.7 0.0 collective-permute-done.ynear_ref
  14.7 1.5 %collective-permute-done.1.yfar_ref = bf16[1,4,64,128]{3,2,1,0:T(8,128)(2,1)S(1)} collective-permute-done((bf16[1,4,64,128]{3,2,1,0:T(8,128)(2,1)S(1)}, bf16[1,4,64,128]{3,2,1,0:T(8,128)(2,1)S(1)}, u32[]{:S(2)}, u32[]{:S(2)}) %collective-permute-start.1) | collective-permute-done | bytes 65568 | tf_op jit(solution)/shard_map/ppermute | solution.py:26
  16.3 1.9 %collective-permute-start.2 = (bf16[6,1,64,128]{3,2,1,0:T(8,128)(2,1)S(1)}, bf16[6,1,64,128]{3,2,1,0:T(8,128)(2,1)S(1)}, u32[]{:S(2)}, u32[]{:S(2)}) collective-permute-start(bf16[6,1,64,128]{3,2,1,0:T(8,128)(2,1)S(1)} %pad_maximum_fusion), channel_id=1, source_target_pairs={{0,16},{16,0},{32,48},{48,32},{64,80},{80,64},{96,112},{112,96},{1... | collective-permute-start | bytes 294920 | tf_op jit(solution)/shard_map/ppermute | solution.py:26
  18.2 0.7 %collective-permute-start.3 = (bf16[6,1,64,128]{3,2,1,0:T(8,128)(2,1)S(1)}, bf16[6,1,64,128]{3,2,1,0:T(8,128)(2,1)S(1)}, u32[]{:S(2)}, u32[]{:S(2)}) collective-permute-start(bf16[6,1,64,128]{3,2,1,0:T(8,128)(2,1)S(1)} %pad_maximum_fusion.1), channel_id=1, source_target_pairs={{16,32},{32,16},{48,64},{64,48},{80,96},{96,80},{112,128},{128,112... | collective-permute-start | bytes 294920 | tf_op jit(solution)/shard_map/ppermute | solution.py:26
  18.9 3.5 %inner.1 = (f32[24,128]{1,0:T(8,128)S(1)}, f32[256,256]{1,0:T(8,128)S(1)}) custom-call(bf16[4,4,64,128]{3,2,1,0:T(8,128)(2,1)S(1)} %get-tuple-element.17.f_ref, bf16[1,4,64,128]{3,2,1,0:T(8,128)(2,1)S(1)} %collective-permute-done.ynear_ref, bf16[1,4,64,128]{3,2,1,0:T(8,128)(2,1)S(1)} %collective-permute-done.1.yfar_ref, ...), custom_call_target="tpu_custom_call" | custom-call | flops 2000000000 | bytes 1000000 | tf_op jit(solution)/shard_map/inner/pallas_call | solution.py:274
  22.4 0.0 collective-permute-done.2.znear_ref
  22.4 0.0 collective-permute-done.3.zfar_ref
  22.5 2.8 %outer.1 = (f32[48,128]{1,0:T(8,128)}, bf16[512,128]{1,0:T(8,128)(2,1)S(1)}) custom-call(bf16[4,4,64,128]{3,2,1,0:T(8,128)(2,1)S(1)} %get-tuple-element.17.f_ref, bf16[1,4,64,128]{3,2,1,0:T(8,128)(2,1)S(1)} %collective-permute-done.ynear_ref, bf16[1,4,64,128]{3,2,1,0:T(8,128)(2,1)S(1)} %collective-permute-done.1.yfar_ref, ...), custom_call_target="tpu_custom_call" | custom-call | tf_op jit(solution)/shard_map/outer/pallas_call | solution.py:287
  25.2 10.1 %all_to_all.14 = bf16[8,64,128]{2,1,0:T(8,128)(2,1)S(1)} all-to-all(bf16[8,64,128]{2,1,0:T(8,128)(2,1)S(1)} %bitcast.11), channel_id=1, replica_groups={{0,1,128,129,256,257,384,385},{2,3,130,131,258,259,386,387},{4,5,132,13..., dimensions={0} | all-to-all | bytes 262144 | tf_op jit(solution)/shard_map/all_to_all | solution.py:328
  35.3 26.2 %all_to_all.15 = f32[64,1,128]{2,1,0:T(1,128)S(1)} all-to-all(f32[64,1,128]{2,1,0:T(1,128)S(1)} %bitcast.13), channel_id=1, replica_groups={{0,2,4,6,8,10,12,14,16,18,20,22,24,26,28,30,32,34,36,38,40,42,44,46,48,..., dimensions={0} | all-to-all | bytes 65536 | tf_op jit(solution)/shard_map/all_to_all | solution.py:330
  61.5 0.6 reduce_sum.19
  (5 shorter events, 0.1 us)
Async XLA Ops:
  1.8 12.9 %collective-permute-start = (bf16[1,4,64,128]{3,2,1,0:T(8,128)(2,1)S(1)}, bf16[1,4,64,128]{3,2,1,0:T(8,128)(2,1)S(1)}, u32[]{:S(2)}, u32[]{:S(2)}) collective-permute-start(bf16[1,4,64,128]{3,2,1,0:T(8,128)(2,1)S(1)} %get-tuple-element.18), channel_id=1, source_target_pairs={{0,1},{1,0},{2,3},{3,2},{4,5},{5,4},{6,7},{7,6},{8,9},{9,8},{10,11... | collective-permute-start | bytes 196616 | tf_op jit(solution)/shard_map/ppermute | solution.py:26
  10.6 5.6 %collective-permute-start.1 = (bf16[1,4,64,128]{3,2,1,0:T(8,128)(2,1)S(1)}, bf16[1,4,64,128]{3,2,1,0:T(8,128)(2,1)S(1)}, u32[]{:S(2)}, u32[]{:S(2)}) collective-permute-start(bf16[1,4,64,128]{3,2,1,0:T(8,128)(2,1)S(1)} %get-tuple-element.19), channel_id=1, source_target_pairs={{1,2},{2,1},{3,4},{4,3},{5,6},{6,5},{7,8},{8,7},{9,10},{10,9},{11,... | collective-permute-start | bytes 196616 | tf_op jit(solution)/shard_map/ppermute | solution.py:26
  16.3 6.2 %collective-permute-start.2 = (bf16[6,1,64,128]{3,2,1,0:T(8,128)(2,1)S(1)}, bf16[6,1,64,128]{3,2,1,0:T(8,128)(2,1)S(1)}, u32[]{:S(2)}, u32[]{:S(2)}) collective-permute-start(bf16[6,1,64,128]{3,2,1,0:T(8,128)(2,1)S(1)} %pad_maximum_fusion), channel_id=1, source_target_pairs={{0,16},{16,0},{32,48},{48,32},{64,80},{80,64},{96,112},{112,96},{1... | collective-permute-start | bytes 294920 | tf_op jit(solution)/shard_map/ppermute | solution.py:26
  18.2 4.2 %collective-permute-start.3 = (bf16[6,1,64,128]{3,2,1,0:T(8,128)(2,1)S(1)}, bf16[6,1,64,128]{3,2,1,0:T(8,128)(2,1)S(1)}, u32[]{:S(2)}, u32[]{:S(2)}) collective-permute-start(bf16[6,1,64,128]{3,2,1,0:T(8,128)(2,1)S(1)} %pad_maximum_fusion.1), channel_id=1, source_target_pairs={{16,32},{32,16},{48,64},{64,48},{80,96},{96,80},{112,128},{128,112... | collective-permute-start | bytes 294920 | tf_op jit(solution)/shard_map/ppermute | solution.py:26

commit v4 on v3

--- a/solution.py
+++ b/solution.py
@@ -46,16 +46,19 @@
     return jnp.broadcast_to(jnp.sum(jnp.where(down == along, row, 0.0), axis=1, keepdims=True), (size, 128))
 
 
-def arrange_kernel(f_ref, cells_ref, ynear_ref, yfar_ref, znear_ref, zfar_ref, wide, f_v, sem):
-    copy = pltpu.make_async_copy(f_ref, f_v, sem)
-    copy.start()
-    copy.wait()
-    wide[...] = f_v[...].astype(jnp.float32)
-    cells = {}
-    for y in range(CORE):
-        for z in range(CORE):
-            cells[y, z] = wide[pl.ds(z * CORE + y, 64, stride=16), :].astype(jnp.bfloat16)
-            cells_ref[y, z] = cells[y, z]
+def arrange_kernel(f_ref, cells_ref, ynear_ref, yfar_ref, znear_ref, zfar_ref, wide, f_v, sems):
+    parts = [slice(i * 256, i * 256 + 256) for i in range(4)]
+    copies = [pltpu.make_async_copy(f_ref.at[part], f_v.at[part], sems.at[i]) for i, part in enumerate(parts)]
+    for copy in copies:
+        copy.start()
+    for i, part in enumerate(parts):
+        copies[i].wait()
+        wide[part] = f_v[part].astype(jnp.float32)
+        for y in range(CORE):
+            for z in range(CORE):
+                piece = wide[pl.ds(i * 256 + z * CORE + y, 16, stride=16), :].astype(jnp.bfloat16)
+                cells_ref[y, z, i * 16 : i * 16 + 16] = piece
+    cells = cells_ref
     last = CORE - 1
     even = is_even("xy")
     for z in range(CORE):
@@ -69,8 +72,8 @@
 
 def prepare_kernel(
     ids_hbm, bins_hbm, map_hbm, taps_hbm, cb_hbm, hb_hbm, hw_hbm,
-    a_ref, col_ref, w_ref, bias_ref, off_ref, hw_ref,
-    ids_ref, bins_ref, map_ref, taps_ref, cb_ref, hb_ref, row_ref, sems,
+    a_ref, col_ref, w_ref, bias_ref, off_ref, heads_ref,
+    ids_ref, bins_ref, map_ref, taps_ref, cb_ref, hb_ref, hw_ref, row_ref, sems,
 ):
     pairs = (
         (ids_hbm, ids_ref), (map_hbm, map_ref), (bins_hbm, bins_ref), (taps_hbm, taps_ref), (cb_hbm, cb_ref),
@@ -111,9 +114,13 @@
         w_ref[64 * dx : 64 * dx + 64, 640:1024] = rows[:, 192:]
     bias_ref[...] = column_of(cb_ref[...], 64)
     off_ref[...] = column_of(hb_ref[...], 8)
-
-
-def predictions(zs, cell, w_ref, bias_ref, hw_ref, hb_ref, g_ref):
+    head = jnp.concatenate([hw_ref[...].astype(jnp.float32), jnp.zeros((5, 64), jnp.float32)], axis=0)
+    blank = jnp.zeros((8, 64), jnp.float32)
+    lines = [jnp.concatenate([head if u == v else blank for u in range(4)], axis=1) for v in range(4)]
+    heads_ref[...] = jnp.concatenate(lines, axis=0).astype(jnp.bfloat16)
+
+
+def predictions(zs, cell, w_ref, bias_ref, heads_ref, hb_ref, g_ref):
     width = 128 * len(zs)
     zero = jnp.zeros((64, 128), jnp.bfloat16)
     for y in range(6):
@@ -129,7 +136,7 @@
     def matmul(left, right):
         return lax.dot_general(left, right, (((1,), (0,)), ((), ())), preferred_element_type=jnp.float32)
 
-    def finish(yv, start, p):
+    def activate(p):
         hidden = []
         for half in range(2):
             q = p[:, half * 128 : half * 128 + 128]
@@ -137,21 +144,37 @@
             after = jnp.where(lane == 127, 0.0, pltpu.roll(q[128:], 127, 1))
             pre = before + q[64:128] + after
             hidden.append(jnp.maximum(pre + bias, 0.0).astype(jnp.bfloat16))
-        logits = matmul(hw_ref[...], jnp.concatenate(hidden, axis=1))
-        for half in range(2):
-            logit = logits[:, half * 128 : half * 128 + 128] + hb_ref[:3]
-            preds[zs[start // 128 + half], yv] = jax.nn.sigmoid(logit)
-
+        return jnp.concatenate(hidden, axis=1)
+
+    def head(batch):
+        hidden = jnp.concatenate([h for _, _, h in batch], axis=0)
+        rows = len(batch)
+        logits = matmul(heads_ref[: 8 * rows, : 64 * rows], hidden)
+        for i, (yv, start, _) in enumerate(batch):
+            for half in range(2):
+                logit = logits[i * 8 : i * 8 + 3, half * 128 : half * 128 + 128] + hb_ref[:3]
+                preds[zs[start // 128 + half], yv] = jax.nn.sigmoid(logit)
+
+    batch = []
     for start in range(0, width, 256):
         cols = slice(start, start + 256)
-        finish(0, start, matmul(w_ref[:, :576], g_ref[:576, cols]))
+
+        def finish(yv, p):
+            batch.append((yv, start, activate(p)))
+            if len(batch) == 4:
+                head(batch)
+                batch.clear()
+
+        finish(0, matmul(w_ref[:, :576], g_ref[:576, cols]))
         cut = matmul(w_ref[:, :384], g_ref[192:576, cols])
-        finish(2, start, cut)
-        finish(1, start, cut + matmul(w_ref[:, 832:1024], g_ref[576:768, cols]))
+        finish(2, cut)
+        finish(1, cut + matmul(w_ref[:, 832:1024], g_ref[576:768, cols]))
         cut = matmul(w_ref[:, 640:1024], g_ref[576:960, cols])
-        finish(3, start, cut)
-        finish(4, start, cut + matmul(w_ref[:, :192], g_ref[384:576, cols]))
-        finish(5, start, matmul(w_ref[:, :576], g_ref[576:1152, cols]))
+        finish(3, cut)
+        finish(4, cut + matmul(w_ref[:, :192], g_ref[384:576, cols]))
+        finish(5, matmul(w_ref[:, :576], g_ref[576:1152, cols]))
+    if batch:
+        head(batch)
     return preds
 
 
@@ -189,21 +212,21 @@
 
 
 def inner_kernel(
-    f_ref, ynear_ref, yfar_ref, w_ref, bias_ref, hw_ref, hb_ref, a_ref, col_ref, part_ref, counts_ref, g_ref, b_ref
+    f_ref, yfar_ref, ynear_ref, w_ref, bias_ref, heads_ref, hb_ref, a_ref, col_ref, part_ref, counts_ref, g_ref, b_ref
 ):
     ylow, yhigh = edges(ynear_ref, yfar_ref, "xy")
 
     def cell(y, z):
         return ylow(0, z - 1) if y == 0 else (yhigh(0, z - 1) if y == 5 else f_ref[y - 1, z - 1])
 
-    blends = blend(predictions(INNER, cell, w_ref, bias_ref, hw_ref, hb_ref, g_ref))
+    blends = blend(predictions(INNER, cell, w_ref, bias_ref, heads_ref, hb_ref, g_ref))
     for i, (axis, at) in enumerate(INNER_ROWS):
         part_ref[i : i + 1] = blends[at][axis : axis + 1]
     counts_ref[...] = histogram(INNER_ROWS, part_ref, col_ref, a_ref[:, : 24 * 128], b_ref)
 
 
 def outer_kernel(
-    f_ref, ynear_ref, yfar_ref, znear_ref, zfar_ref, w_ref, bias_ref, hw_ref, hb_ref, a_ref, col_ref, part_ref, counts_ref,
+    f_ref, yfar_ref, ynear_ref, zfar_ref, znear_ref, w_ref, bias_ref, heads_ref, hb_ref, a_ref, col_ref, part_ref, counts_ref,
     out_ref, table_ref, g_ref, b_ref, value_ref,
 ):
     ylow, yhigh = edges(ynear_ref, yfar_ref, "xy")
@@ -214,7 +237,7 @@
             return (zlow if z == 0 else zhigh)(y, 0)
         return ylow(0, z - 1) if y == 0 else (yhigh(0, z - 1) if y == 5 else f_ref[y - 1, z - 1])
 
-    blends = blend(predictions(OUTER, cell, w_ref, bias_ref, hw_ref, hb_ref, g_ref))
+    blends = blend(predictions(OUTER, cell, w_ref, bias_ref, heads_ref, hb_ref, g_ref))
     for i, (axis, at) in enumerate(OUTER_ROWS):
         value_ref[i : i + 1] = blends[at][axis : axis + 1]
     for axis in range(3):
@@ -246,7 +269,7 @@
         in_specs=[pl.BlockSpec(memory_space=pltpu.HBM)],
         out_specs=tuple(vmem(5)),
         scratch_shapes=[
-            pltpu.VMEM((1024, 128), jnp.float32), pltpu.VMEM((1024, 128), jnp.bfloat16), pltpu.SemaphoreType.DMA(()),
+            pltpu.VMEM((1024, 128), jnp.float32), pltpu.VMEM((1024, 128), jnp.bfloat16), pltpu.SemaphoreType.DMA((4,)),
         ],
         compiler_params=pltpu.CompilerParams(vmem_limit_bytes=VMEM_LIMIT),
         name="arrange",
@@ -258,11 +281,11 @@
         prepare_kernel,
         out_shape=(
             shape((256, 6144), jnp.bfloat16), shape((48, 128), jnp.float32), shape((192, 1024), jnp.bfloat16),
-            shape((64, 128), jnp.float32), shape((8, 128), jnp.float32), shape((3, 64), jnp.bfloat16),
+            shape((64, 128), jnp.float32), shape((8, 128), jnp.float32), shape((32, 256), jnp.bfloat16),
         ),
         in_specs=[pl.BlockSpec(memory_space=pltpu.HBM)] * 7,
         out_specs=tuple(vmem(6)),
-        scratch_shapes=[pltpu.VMEM(o.shape, o.dtype) for o in operands[:-1]]
+        scratch_shapes=[pltpu.VMEM(o.shape, o.dtype) for o in operands]
         + [pltpu.VMEM((48, 128), jnp.float32), pltpu.SemaphoreType.DMA((7,))],
         compiler_params=pltpu.CompilerParams(vmem_limit_bytes=VMEM_LIMIT),
         cost_estimate=pl.CostEstimate(flops=10**9, bytes_accessed=10**7, transcendentals=0),
@@ -298,6 +321,22 @@
     )(*operands)
 
 
+def finish_kernel(values_ref, sums_ref, out_ref, share_ref):
+    out_ref[...] = values_ref[...]
+    share_ref[...] = jnp.sum(sums_ref[...], axis=0, keepdims=True)
+
+
+def finish(*operands):
+    return pl.pallas_call(
+        finish_kernel,
+        out_shape=(shape((48, 128), jnp.float32), shape((1, 128), jnp.float32)),
+        in_specs=vmem(2),
+        out_specs=tuple(vmem(2)),
+        compiler_params=pltpu.CompilerParams(vmem_limit_bytes=2 * 1024 * 1024),
+        name="finish",
+    )(*operands)
+
+
 def groups(kept):
     ids = np.arange(512).reshape(4, 8, 8, 2)
     return ids.transpose(1, 2, 0, 3).reshape(64, 8).tolist() if kept == "xc" else ids.transpose(0, 3, 1, 2).reshape(8, 64).tolist()
@@ -320,15 +359,15 @@
         return jnp.concatenate([low, face, high], axis=0)
 
     znear, zfar = swaps("gz", with_corners(znear, zeven), with_corners(zfar, jnp.logical_not(zeven)))
-    part, counts = inner(cells, ynear, yfar, weights, bias, heads, offset, owners, columns)
+    part, counts = inner(cells, yfar, ynear, weights, bias, heads, offset, owners, columns)
     blended, table = outer(
-        cells, ynear, yfar, znear, zfar, weights, bias, heads, offset, owners, columns, part, counts
+        cells, yfar, ynear, zfar, znear, weights, bias, heads, offset, owners, columns, part, counts
     )
     every = ("gz", "xy")
     parts = lax.all_to_all(table.reshape(8, 64, 128), every, 0, 0, tiled=True, axis_index_groups=groups("xc"))
     sums = jnp.sum(parts.astype(jnp.float32), axis=0)
     sums = lax.all_to_all(sums, every, 0, 0, tiled=True, axis_index_groups=groups("yz"))
-    share = jnp.sum(sums, axis=0, keepdims=True)
+    blended, share = finish(blended, sums)
     return blended.reshape(3, CORE, CORE, 128), share
 
 

time: 62.4 us -> 59 us (0.946)
  Pallas kernels: 9.62 us -> 7.87 us
  waiting for transfers between devices: 1.49 us -> 0.13 us
    all_to_all x1, blocking collectives: 26.2 us -> 23.1 us  [on_device(): lax.all_to_all(sums, every, 0, 0, tiled=True, axis_index_groups=groups('y...]
    all_to_all x1, blocking collectives: 10.1 us -> 13 us  [on_device(): lax.all_to_all(table.reshape(8, 64, 128), every, 0, 0, tiled=True, axis_i...]
    ppermute x4, waiting for transfers between devices: 1.49 us -> 0.13 us  [swaps(): return (lax.ppermute(inside, axis, near), lax.ppermute(outside, axis, far))]
    pallas_call x1, Pallas kernels: 3.54 us -> 2.24 us  [inner(): pl.pallas_call(inner_kernel, out_shape=(shape((24, 128), jnp.float32), sh...]
    pallas_call x1, Pallas kernels: 2.77 us -> 1.74 us  [outer(): pl.pallas_call(outer_kernel, out_shape=(shape((48, 128), jnp.float32), sh...]
  transfers between devices with their start and end apart: 4 -> 4, of which waited for: 1 -> 1; matrix products, arithmetic and copies ran while one was open for 0% -> 0% of each run, Pallas kernels for 9% -> 7%
where the time goes in v4:
time: 59 us; the launch traced here: 58.7 us
  blocking collectives  36.1 us (61%)
  starting transfers between devices  13.7 us (23%)
  Pallas kernels  7.87 us (13%)
  between operations  0.77 us (1%)
    all_to_all x1, blocking collectives, on_device(): lax.all_to_all(sums, every, 0, 0, tiled=True, axis_index_groups=groups('y...  23.1 us
    ppermute x4, starting transfers between devices, swaps(): return (lax.ppermute(inside, axis, near), lax.ppermute(outside, axis, far))  13.7 us
    all_to_all x1, blocking collectives, on_device(): lax.all_to_all(table.reshape(8, 64, 128), every, 0, 0, tiled=True, axis_i...  13 us
    pallas_call x1, Pallas kernels, inner(): pl.pallas_call(inner_kernel, out_shape=(shape((24, 128), jnp.float32), sh...  2.24 us
    pallas_call x1, Pallas kernels, prepare(): pl.pallas_call(prepare_kernel, out_shape=(shape((256, 6144), jnp.bfloat16...  2.14 us
    pallas_call x1, Pallas kernels, outer(): pl.pallas_call(outer_kernel, out_shape=(shape((48, 128), jnp.float32), sh...  1.74 us
  transfers between devices with their start and end apart: 4, of which 1 were waited for; matrix products, arithmetic and copies ran while one was open for 0% of the time, Pallas kernels for 7%

profile of v4, /device:TPU:1, one launch (start us, length us, event | category | flops | bytes accessed | tf_op | source)
XLA Modules:
  0.0 58.7 jit_solution(12400688288049630755)
XLA Ops:
  0.6 1.1 %arrange.1 = (bf16[4,4,64,128]{3,2,1,0:T(8,128)(2,1)S(1)}, bf16[1,4,64,128]{3,2,1,0:T(8,128)(2,1)S(1)}, bf16[1,4,64,128]{3,2,1,0:T(8,128)(2,1)S(1)}, bf16[4,1,64...) custom-call(bf16[1024,128]{1,0:T(8,128)(2,1)} %bitcast.13), custom_call_target="tpu_custom_call" | custom-call | tf_op jit(solution)/shard_map/arrange/pallas_call | solution.py:266
  1.8 5.4 %collective-permute-start = (bf16[1,4,64,128]{3,2,1,0:T(8,128)(2,1)S(1)}, bf16[1,4,64,128]{3,2,1,0:T(8,128)(2,1)S(1)}, u32[]{:S(2)}, u32[]{:S(2)}) collective-permute-start(bf16[1,4,64,128]{3,2,1,0:T(8,128)(2,1)S(1)} %get-tuple-element.20), channel_id=1, source_target_pairs={{1,2},{2,1},{3,4},{4,3},{5,6},{6,5},{7,8},{8,7},{9,10},{10,9},{11,... | collective-permute-start | bytes 196616 | tf_op jit(solution)/shard_map/ppermute | solution.py:26
  7.2 4.1 %collective-permute-start.1 = (bf16[1,4,64,128]{3,2,1,0:T(8,128)(2,1)S(1)}, bf16[1,4,64,128]{3,2,1,0:T(8,128)(2,1)S(1)}, u32[]{:S(2)}, u32[]{:S(2)}) collective-permute-start(bf16[1,4,64,128]{3,2,1,0:T(8,128)(2,1)S(1)} %get-tuple-element.21), channel_id=1, source_target_pairs={{0,1},{1,0},{2,3},{3,2},{4,5},{5,4},{6,7},{7,6},{8,9},{9,8},{10,11... | collective-permute-start | bytes 196616 | tf_op jit(solution)/shard_map/ppermute | solution.py:26
  11.3 2.1 %prepare.1 = (bf16[256,6144]{1,0:T(8,128)(2,1)S(1)}, f32[48,128]{1,0:T(8,128)S(1)}, bf16[192,1024]{1,0:T(8,128)(2,1)S(1)}, f32[64,128]{1,0:T(8,128)S(1)}, f32[8,...) custom-call(s32[48,128]{1,0:T(8,128)} %bitcast.16, s32[16,128]{1,0:T(8,128)} %bitcast.19, s32[32,128]{1,0:T(8,128)} %bitcast.18, ...), custom_call_target="tpu_custom_call" | custom-call | flops 1000000000 | bytes 10000000 | tf_op jit(solution)/shard_map/prepare/pallas_call | solution.py:280
  13.4 0.0 collective-permute-done.yfar_ref
  13.4 0.0 collective-permute-done.1.ynear_ref
  13.5 0.7 %collective-permute-start.2 = (bf16[6,1,64,128]{3,2,1,0:T(8,128)(2,1)S(1)}, bf16[6,1,64,128]{3,2,1,0:T(8,128)(2,1)S(1)}, u32[]{:S(2)}, u32[]{:S(2)}) collective-permute-start(bf16[6,1,64,128]{3,2,1,0:T(8,128)(2,1)S(1)} %pad_maximum_fusion), channel_id=1, source_target_pairs={{16,32},{32,16},{48,64},{64,48},{80,96},{96,80},{112,128},{128,112... | collective-permute-start | bytes 294920 | tf_op jit(solution)/shard_map/ppermute | solution.py:26
  14.2 3.6 %collective-permute-start.3 = (bf16[6,1,64,128]{3,2,1,0:T(8,128)(2,1)S(1)}, bf16[6,1,64,128]{3,2,1,0:T(8,128)(2,1)S(1)}, u32[]{:S(2)}, u32[]{:S(2)}) collective-permute-start(bf16[6,1,64,128]{3,2,1,0:T(8,128)(2,1)S(1)} %pad_maximum_fusion.1), channel_id=1, source_target_pairs={{0,16},{16,0},{32,48},{48,32},{64,80},{80,64},{96,112},{112,96},{1... | collective-permute-start | bytes 294920 | tf_op jit(solution)/shard_map/ppermute | solution.py:26
  17.8 2.2 %inner.1 = (f32[24,128]{1,0:T(8,128)S(1)}, f32[256,256]{1,0:T(8,128)S(1)}) custom-call(bf16[4,4,64,128]{3,2,1,0:T(8,128)(2,1)S(1)} %get-tuple-element.19.f_ref, bf16[1,4,64,128]{3,2,1,0:T(8,128)(2,1)S(1)} %collective-permute-done.yfar_ref, bf16[1,4,64,128]{3,2,1,0:T(8,128)(2,1)S(1)} %collective-permute-done.1.ynear_ref, ...), custom_call_target="tpu_custom_call" | custom-call | flops 2000000000 | bytes 1000000 | tf_op jit(solution)/shard_map/inner/pallas_call | solution.py:297
  20.1 0.0 collective-permute-done.2.zfar_ref
  20.1 0.1 collective-permute-done.3.znear_ref
  20.2 1.7 %outer.1 = (f32[48,128]{1,0:T(8,128)S(1)}, bf16[512,128]{1,0:T(8,128)(2,1)S(1)}) custom-call(bf16[4,4,64,128]{3,2,1,0:T(8,128)(2,1)S(1)} %get-tuple-element.19.f_ref, bf16[1,4,64,128]{3,2,1,0:T(8,128)(2,1)S(1)} %collective-permute-done.yfar_ref, bf16[1,4,64,128]{3,2,1,0:T(8,128)(2,1)S(1)} %collective-permute-done.1.ynear_ref, ...), custom_call_target="tpu_custom_call" | custom-call | tf_op jit(solution)/shard_map/outer/pallas_call | solution.py:310
  21.9 13.0 %all_to_all.16 = bf16[8,64,128]{2,1,0:T(8,128)(2,1)S(1)} all-to-all(bf16[8,64,128]{2,1,0:T(8,128)(2,1)S(1)} %bitcast.12), channel_id=1, replica_groups={{0,1,128,129,256,257,384,385},{2,3,130,131,258,259,386,387},{4,5,132,13..., dimensions={0} | all-to-all | bytes 262144 | tf_op jit(solution)/shard_map/all_to_all | solution.py:367
  34.9 23.1 %all_to_all.17 = f32[64,1,128]{2,1,0:T(1,128)S(1)} all-to-all(f32[64,1,128]{2,1,0:T(1,128)S(1)} %bitcast.14), channel_id=1, replica_groups={{0,2,4,6,8,10,12,14,16,18,20,22,24,26,28,30,32,34,36,38,40,42,44,46,48,..., dimensions={0} | all-to-all | bytes 65536 | tf_op jit(solution)/shard_map/all_to_all | solution.py:369
  58.1 0.6 %finish.1 = (f32[48,128]{1,0:T(8,128)}, f32[1,128]{1,0:T(1,128)}) custom-call(f32[48,128]{1,0:T(8,128)S(1)} %get-tuple-element.32.values_ref, f32[64,128]{1,0:T(8,128)S(1)} %bitcast.11), custom_call_target="tpu_custom_call" | custom-call | tf_op jit(solution)/shard_map/finish/pallas_call | solution.py:330
  (5 shorter events, 0.1 us)
Async XLA Ops:
  1.8 11.6 %collective-permute-start = (bf16[1,4,64,128]{3,2,1,0:T(8,128)(2,1)S(1)}, bf16[1,4,64,128]{3,2,1,0:T(8,128)(2,1)S(1)}, u32[]{:S(2)}, u32[]{:S(2)}) collective-permute-start(bf16[1,4,64,128]{3,2,1,0:T(8,128)(2,1)S(1)} %get-tuple-element.20), channel_id=1, source_target_pairs={{1,2},{2,1},{3,4},{4,3},{5,6},{6,5},{7,8},{8,7},{9,10},{10,9},{11,... | collective-permute-start | bytes 196616 | tf_op jit(solution)/shard_map/ppermute | solution.py:26
  7.2 6.2 %collective-permute-start.1 = (bf16[1,4,64,128]{3,2,1,0:T(8,128)(2,1)S(1)}, bf16[1,4,64,128]{3,2,1,0:T(8,128)(2,1)S(1)}, u32[]{:S(2)}, u32[]{:S(2)}) collective-permute-start(bf16[1,4,64,128]{3,2,1,0:T(8,128)(2,1)S(1)} %get-tuple-element.21), channel_id=1, source_target_pairs={{0,1},{1,0},{2,3},{3,2},{4,5},{5,4},{6,7},{7,6},{8,9},{9,8},{10,11... | collective-permute-start | bytes 196616 | tf_op jit(solution)/shard_map/ppermute | solution.py:26
  13.5 6.6 %collective-permute-start.2 = (bf16[6,1,64,128]{3,2,1,0:T(8,128)(2,1)S(1)}, bf16[6,1,64,128]{3,2,1,0:T(8,128)(2,1)S(1)}, u32[]{:S(2)}, u32[]{:S(2)}) collective-permute-start(bf16[6,1,64,128]{3,2,1,0:T(8,128)(2,1)S(1)} %pad_maximum_fusion), channel_id=1, source_target_pairs={{16,32},{32,16},{48,64},{64,48},{80,96},{96,80},{112,128},{128,112... | collective-permute-start | bytes 294920 | tf_op jit(solution)/shard_map/ppermute | solution.py:26
  14.2 6.0 %collective-permute-start.3 = (bf16[6,1,64,128]{3,2,1,0:T(8,128)(2,1)S(1)}, bf16[6,1,64,128]{3,2,1,0:T(8,128)(2,1)S(1)}, u32[]{:S(2)}, u32[]{:S(2)}) collective-permute-start(bf16[6,1,64,128]{3,2,1,0:T(8,128)(2,1)S(1)} %pad_maximum_fusion.1), channel_id=1, source_target_pairs={{0,16},{16,0},{32,48},{48,32},{64,80},{80,64},{96,112},{112,96},{1... | collective-permute-start | bytes 294920 | tf_op jit(solution)/shard_map/ppermute | solution.py:26

commit v5 on v4

--- a/solution.py
+++ b/solution.py
@@ -9,10 +9,13 @@
 BINS = 16
 CORE = 4
 TAPS = 3
+SMALL = 6
 FULL = (0, 1, 2)
 VMEM_LIMIT = 32 * 1024 * 1024
 
 VARIANTS = ((0, FULL), (1, FULL), (1, (0, 1)), (2, (1, 2)), (2, FULL), (3, FULL))
+FIELDS = {"x": (7, 2), "y": (4, 3), "z": (1, 3), "c": (0, 1)}
+EXCHANGES = ("xc", "yz")
 INNER = (1, 2, 3, 4)
 OUTER = (0, 5)
 INNER_ROWS = [(axis, at) for axis in range(3) for at in range(4, 12)]
@@ -46,9 +49,13 @@
     return jnp.broadcast_to(jnp.sum(jnp.where(down == along, row, 0.0), axis=1, keepdims=True), (size, 128))
 
 
-def arrange_kernel(f_ref, cells_ref, ynear_ref, yfar_ref, znear_ref, zfar_ref, wide, f_v, sems):
+def arrange_kernel(f_ref, *refs):
+    sources, refs = refs[:SMALL], refs[SMALL:]
+    (cells_ref, ynear_ref, yfar_ref, znear_ref, zfar_ref), refs = refs[:5], refs[5:]
+    targets, (wide, f_v, sems) = refs[:SMALL], refs[SMALL:]
     parts = [slice(i * 256, i * 256 + 256) for i in range(4)]
     copies = [pltpu.make_async_copy(f_ref.at[part], f_v.at[part], sems.at[i]) for i, part in enumerate(parts)]
+    copies += [pltpu.make_async_copy(src, dst, sems.at[4 + i]) for i, (src, dst) in enumerate(zip(sources, targets))]
     for copy in copies:
         copy.start()
     for i, part in enumerate(parts):
@@ -68,22 +75,31 @@
     for y in range(CORE):
         znear_ref[y, 0] = jnp.where(even, cells[y, last], cells[y, 0])
         zfar_ref[y, 0] = jnp.where(even, cells[y, 0], cells[y, last])
+    for copy in copies[4:]:
+        copy.wait()
 
 
 def prepare_kernel(
-    ids_hbm, bins_hbm, map_hbm, taps_hbm, cb_hbm, hb_hbm, hw_hbm,
-    a_ref, col_ref, w_ref, bias_ref, off_ref, heads_ref,
-    ids_ref, bins_ref, map_ref, taps_ref, cb_ref, hb_ref, hw_ref, row_ref, sems,
+    taps_hbm, cb_ref, hb_ref, hw_ref, ids_ref, bins_ref, map_ref, w_ref, bias_ref, off_ref, heads_ref, a_ref, col_ref,
+    row_ref, taps_ref, sem,
 ):
-    pairs = (
-        (ids_hbm, ids_ref), (map_hbm, map_ref), (bins_hbm, bins_ref), (taps_hbm, taps_ref), (cb_hbm, cb_ref),
-        (hb_hbm, hb_ref), (hw_hbm, hw_ref),
-    )
-    copies = [pltpu.make_async_copy(src, dst, sems.at[i]) for i, (src, dst) in enumerate(pairs)]
-    for copy in copies:
-        copy.start()
-    for copy in copies:
-        copy.wait()
+    fetch = pltpu.make_async_copy(taps_hbm, taps_ref, sem)
+    fetch.start()
+    lookup(ids_ref, bins_ref, map_ref, a_ref, col_ref, row_ref)
+    fetch.wait()
+    for dx in range(TAPS):
+        rows = jnp.concatenate([taps_ref[t % 3, t // 3, dx] for t in range(9)], axis=1)
+        w_ref[64 * dx : 64 * dx + 64, :576] = rows
+        w_ref[64 * dx : 64 * dx + 64, 640:1024] = rows[:, 192:]
+    bias_ref[...] = column_of(cb_ref[...], 64)
+    off_ref[...] = column_of(hb_ref[...], 8)
+    head = jnp.concatenate([hw_ref[...].astype(jnp.float32), jnp.zeros((5, 64), jnp.float32)], axis=0)
+    blank = jnp.zeros((8, 64), jnp.float32)
+    lines = [jnp.concatenate([head if u == v else blank for u in range(4)], axis=1) for v in range(4)]
+    heads_ref[...] = jnp.concatenate(lines, axis=0).astype(jnp.bfloat16)
+
+
+def lookup(ids_ref, bins_ref, map_ref, a_ref, col_ref, row_ref):
     one = jnp.ones((), jnp.bfloat16)
     none = jnp.zeros((), jnp.bfloat16)
     bins = bins_ref[...]
@@ -98,7 +114,11 @@
             line = jnp.broadcast_to(map_ref[h : h + 1], (8, 128))
             slot = jnp.where(high == h, jnp.take_along_axis(line, low, axis=1, mode="promise_in_bounds"), slot)
         owner = slot >> 3
-        place = (owner & 384) + ((owner & 1) << 6) + ((owner >> 1) & 63)
+        place, shift = 0, 9
+        for axis in "".join(EXCHANGES):
+            low, width = FIELDS[axis]
+            shift -= width
+            place += ((owner >> low) & (2**width - 1)) << shift
         first = block % 2 * 8
         column = (place >> 8) * 128 + (slot & 7) * BINS + bins[first : first + 8]
         col_ref[rows] = jnp.where(ids >= 0, column, -1).astype(jnp.float32)
@@ -108,16 +128,6 @@
         r = axis * 16 + at
         row = row_ref[r : r + 1].astype(jnp.bfloat16)
         a_ref[:, i * 128 : i * 128 + 128] = jnp.where(count == row, one, none)
-    for dx in range(TAPS):
-        rows = jnp.concatenate([taps_ref[t % 3, t // 3, dx] for t in range(9)], axis=1)
-        w_ref[64 * dx : 64 * dx + 64, :576] = rows
-        w_ref[64 * dx : 64 * dx + 64, 640:1024] = rows[:, 192:]
-    bias_ref[...] = column_of(cb_ref[...], 64)
-    off_ref[...] = column_of(hb_ref[...], 8)
-    head = jnp.concatenate([hw_ref[...].astype(jnp.float32), jnp.zeros((5, 64), jnp.float32)], axis=0)
-    blank = jnp.zeros((8, 64), jnp.float32)
-    lines = [jnp.concatenate([head if u == v else blank for u in range(4)], axis=1) for v in range(4)]
-    heads_ref[...] = jnp.concatenate(lines, axis=0).astype(jnp.bfloat16)
 
 
 def predictions(zs, cell, w_ref, bias_ref, heads_ref, hb_ref, g_ref):
@@ -261,36 +271,37 @@
     return pltpu.with_memory_space_constraint(array, pltpu.HBM)
 
 
-def arrange(features):
+def arrange(*operands):
     yface, zface = shape((1, CORE, 64, 128), jnp.bfloat16), shape((CORE, 1, 64, 128), jnp.bfloat16)
+    small = tuple(shape(o.shape, o.dtype) for o in operands[1:])
     return pl.pallas_call(
         arrange_kernel,
-        out_shape=(shape((CORE, CORE, 64, 128), jnp.bfloat16), yface, yface, zface, zface),
-        in_specs=[pl.BlockSpec(memory_space=pltpu.HBM)],
-        out_specs=tuple(vmem(5)),
+        out_shape=(shape((CORE, CORE, 64, 128), jnp.bfloat16), yface, yface, zface, zface) + small,
+        in_specs=[pl.BlockSpec(memory_space=pltpu.HBM)] * (1 + SMALL),
+        out_specs=tuple(vmem(5 + SMALL)),
         scratch_shapes=[
-            pltpu.VMEM((1024, 128), jnp.float32), pltpu.VMEM((1024, 128), jnp.bfloat16), pltpu.SemaphoreType.DMA((4,)),
+            pltpu.VMEM((1024, 128), jnp.float32), pltpu.VMEM((1024, 128), jnp.bfloat16),
+            pltpu.SemaphoreType.DMA((4 + SMALL,)),
         ],
         compiler_params=pltpu.CompilerParams(vmem_limit_bytes=VMEM_LIMIT),
         name="arrange",
-    )(in_hbm(features))
-
-
-def prepare(*operands):
+    )(*map(in_hbm, operands))
+
+
+def prepare(taps, *operands):
     return pl.pallas_call(
         prepare_kernel,
         out_shape=(
-            shape((256, 6144), jnp.bfloat16), shape((48, 128), jnp.float32), shape((192, 1024), jnp.bfloat16),
-            shape((64, 128), jnp.float32), shape((8, 128), jnp.float32), shape((32, 256), jnp.bfloat16),
+            shape((192, 1024), jnp.bfloat16), shape((64, 128), jnp.float32), shape((8, 128), jnp.float32),
+            shape((32, 256), jnp.bfloat16), shape((256, 6144), jnp.bfloat16), shape((48, 128), jnp.float32),
         ),
-        in_specs=[pl.BlockSpec(memory_space=pltpu.HBM)] * 7,
+        in_specs=[pl.BlockSpec(memory_space=pltpu.HBM)] + vmem(6),
         out_specs=tuple(vmem(6)),
-        scratch_shapes=[pltpu.VMEM(o.shape, o.dtype) for o in operands]
-        + [pltpu.VMEM((48, 128), jnp.float32), pltpu.SemaphoreType.DMA((7,))],
+        scratch_shapes=[pltpu.VMEM((48, 128), jnp.float32), pltpu.VMEM(taps.shape, taps.dtype), pltpu.SemaphoreType.DMA(())],
         compiler_params=pltpu.CompilerParams(vmem_limit_bytes=VMEM_LIMIT),
         cost_estimate=pl.CostEstimate(flops=10**9, bytes_accessed=10**7, transcendentals=0),
         name="prepare",
-    )(*map(in_hbm, operands))
+    )(in_hbm(taps), *operands)
 
 
 def inner(*operands):
@@ -338,18 +349,24 @@
 
 
 def groups(kept):
-    ids = np.arange(512).reshape(4, 8, 8, 2)
-    return ids.transpose(1, 2, 0, 3).reshape(64, 8).tolist() if kept == "xc" else ids.transpose(0, 3, 1, 2).reshape(8, 64).tolist()
+    axes = [axis for axis in FIELDS if axis not in kept] + list(kept)
+    ids = np.arange(512).reshape(4, 8, 8, 2).transpose([list(FIELDS).index(axis) for axis in axes])
+    return ids.reshape(-1, members(kept)).tolist()
+
+
+def members(kept):
+    return 2 ** sum(FIELDS[axis][1] for axis in kept)
 
 
 def on_device(features, conv_w, conv_b, head_w, head_b, bins, edge_ids, owner_map):
     last = CORE - 1
-    cells, ynear, yfar, znear, zfar = arrange(features.reshape(1024, 128))
+    cells, ynear, yfar, znear, zfar, ids, bins, owner_map, conv_b, head_b, head_w = arrange(
+        features.reshape(1024, 128), edge_ids.reshape(48, 128), bins.reshape(16, 128), owner_map.reshape(32, 128),
+        conv_b.reshape(1, 64), head_b.reshape(1, 3), head_w,
+    )
     ynear, yfar = swaps("xy", ynear, yfar)
-    owners, columns, weights, bias, offset, heads = prepare(
-        edge_ids.reshape(48, 128), bins.reshape(16, 128), owner_map.reshape(32, 128),
-        jnp.transpose(conv_w, (2, 3, 4, 0, 1)), conv_b.reshape(1, 64), head_b.reshape(1, 3), head_w,
-    )
+    taps = jnp.transpose(conv_w, (2, 3, 4, 0, 1))
+    weights, bias, offset, heads, owners, columns = prepare(taps, conv_b, head_b, head_w, ids, bins, owner_map)
     yeven, zeven = is_even("xy"), is_even("gz")
     ylow, yhigh = jnp.where(yeven, yfar, ynear), jnp.where(yeven, ynear, yfar)
 
@@ -364,9 +381,11 @@
         cells, yfar, ynear, zfar, znear, weights, bias, heads, offset, owners, columns, part, counts
     )
     every = ("gz", "xy")
-    parts = lax.all_to_all(table.reshape(8, 64, 128), every, 0, 0, tiled=True, axis_index_groups=groups("xc"))
+    one, two = EXCHANGES
+    parts = table.reshape(members(one), members(two), 128)
+    parts = lax.all_to_all(parts, every, 0, 0, tiled=True, axis_index_groups=groups(one))
     sums = jnp.sum(parts.astype(jnp.float32), axis=0)
-    sums = lax.all_to_all(sums, every, 0, 0, tiled=True, axis_index_groups=groups("yz"))
+    sums = lax.all_to_all(sums, every, 0, 0, tiled=True, axis_index_groups=groups(two))
     blended, share = finish(blended, sums)
     return blended.reshape(3, CORE, CORE, 128), share
 

time: 59 us -> 58.3 us (0.988)
  Pallas kernels: 7.87 us -> 7.1 us
    pallas_call x1, Pallas kernels: 2.14 us -> 1.29 us  [prepare(): pl.pallas_call(prepare_kernel, out_shape=(shape((192, 1024), jnp.bfloat16...]
  transfers between devices with their start and end apart: 4 -> 4, of which waited for: 1 -> 1; matrix products, arithmetic and copies ran while one was open for 0% -> 0% of each run, Pallas kernels for 7% -> 6%
where the time goes in v5:
time: 58.3 us; the launch traced here: 57.9 us
  blocking collectives  36.1 us (62%)
  starting transfers between devices  13.7 us (23%)
  Pallas kernels  7.1 us (12%)
  between operations  0.78 us (1%)
    all_to_all x1, blocking collectives, on_device(): lax.all_to_all(sums, every, 0, 0, tiled=True, axis_index_groups=groups(two))  23.2 us
    ppermute x4, starting transfers between devices, swaps(): return (lax.ppermute(inside, axis, near), lax.ppermute(outside, axis, far))  13.7 us
    all_to_all x1, blocking collectives, on_device(): lax.all_to_all(parts, every, 0, 0, tiled=True, axis_index_groups=groups(o...  13 us
    pallas_call x1, Pallas kernels, inner(): pl.pallas_call(inner_kernel, out_shape=(shape((24, 128), jnp.float32), sh...  2.25 us
    pallas_call x1, Pallas kernels, outer(): pl.pallas_call(outer_kernel, out_shape=(shape((48, 128), jnp.float32), sh...  1.76 us
    pallas_call x1, Pallas kernels, prepare(): pl.pallas_call(prepare_kernel, out_shape=(shape((192, 1024), jnp.bfloat16...  1.29 us
    pallas_call x1, Pallas kernels, arrange(): pl.pallas_call(arrange_kernel, out_shape=(shape((CORE, CORE, 64, 128), jn...  1.2 us
  transfers between devices with their start and end apart: 4, of which 1 were waited for; matrix products, arithmetic and copies ran while one was open for 0% of the time, Pallas kernels for 6%

profile of v5, /device:TPU:1, one launch (start us, length us, event | category | flops | bytes accessed | tf_op | source)
XLA Modules:
  0.0 57.9 jit_solution(7342143779290156009)
XLA Ops:
  0.6 1.2 %arrange.1 = (bf16[4,4,64,128]{3,2,1,0:T(8,128)(2,1)S(1)}, bf16[1,4,64,128]{3,2,1,0:T(8,128)(2,1)S(1)}, bf16[1,4,64,128]{3,2,1,0:T(8,128)(2,1)S(1)}, bf16[4,1,64...) custom-call(bf16[1024,128]{1,0:T(8,128)(2,1)} %bitcast.13, ...), custom_call_target="tpu_custom_call" | custom-call | tf_op jit(solution)/shard_map/arrange/pallas_call | solution.py:277
  1.8 5.4 %collective-permute-start = (bf16[1,4,64,128]{3,2,1,0:T(8,128)(2,1)S(1)}, bf16[1,4,64,128]{3,2,1,0:T(8,128)(2,1)S(1)}, u32[]{:S(2)}, u32[]{:S(2)}) collective-permute-start(bf16[1,4,64,128]{3,2,1,0:T(8,128)(2,1)S(1)} %get-tuple-element.26), channel_id=1, source_target_pairs={{1,2},{2,1},{3,4},{4,3},{5,6},{6,5},{7,8},{8,7},{9,10},{10,9},{11,... | collective-permute-start | bytes 196616 | tf_op jit(solution)/shard_map/ppermute | solution.py:29
  7.2 4.1 %collective-permute-start.1 = (bf16[1,4,64,128]{3,2,1,0:T(8,128)(2,1)S(1)}, bf16[1,4,64,128]{3,2,1,0:T(8,128)(2,1)S(1)}, u32[]{:S(2)}, u32[]{:S(2)}) collective-permute-start(bf16[1,4,64,128]{3,2,1,0:T(8,128)(2,1)S(1)} %get-tuple-element.27), channel_id=1, source_target_pairs={{0,1},{1,0},{2,3},{3,2},{4,5},{5,4},{6,7},{7,6},{8,9},{9,8},{10,11... | collective-permute-start | bytes 196616 | tf_op jit(solution)/shard_map/ppermute | solution.py:29
  11.3 1.3 %prepare.1 = (bf16[192,1024]{1,0:T(8,128)(2,1)S(1)}, f32[64,128]{1,0:T(8,128)S(1)}, f32[8,128]{1,0:T(8,128)S(1)}, bf16[32,256]{1,0:T(8,128)(2,1)S(1)}, bf16[256,...) custom-call(bf16[3,3,3,64,64]{4,3,2,1,0:T(8,128)(2,1)} %bitcast.20, f32[1,64]{1,0:T(1,128)S(1)} %get-tuple-element.30.cb_ref, ...), custom_call_target="tpu_custom_call" | custom-call | flops 1000000000 | bytes 10000000 | tf_op jit(solution)/shard_map/prepare/pallas_call | solution.py:292
  12.6 0.0 collective-permute-done.yfar_ref
  12.6 0.0 collective-permute-done.1.ynear_ref
  12.7 0.7 %collective-permute-start.2 = (bf16[6,1,64,128]{3,2,1,0:T(8,128)(2,1)S(1)}, bf16[6,1,64,128]{3,2,1,0:T(8,128)(2,1)S(1)}, u32[]{:S(2)}, u32[]{:S(2)}) collective-permute-start(bf16[6,1,64,128]{3,2,1,0:T(8,128)(2,1)S(1)} %pad_maximum_fusion), channel_id=1, source_target_pairs={{16,32},{32,16},{48,64},{64,48},{80,96},{96,80},{112,128},{128,112... | collective-permute-start | bytes 294920 | tf_op jit(solution)/shard_map/ppermute | solution.py:29
  13.4 3.6 %collective-permute-start.3 = (bf16[6,1,64,128]{3,2,1,0:T(8,128)(2,1)S(1)}, bf16[6,1,64,128]{3,2,1,0:T(8,128)(2,1)S(1)}, u32[]{:S(2)}, u32[]{:S(2)}) collective-permute-start(bf16[6,1,64,128]{3,2,1,0:T(8,128)(2,1)S(1)} %pad_maximum_fusion.1), channel_id=1, source_target_pairs={{0,16},{16,0},{32,48},{48,32},{64,80},{80,64},{96,112},{112,96},{1... | collective-permute-start | bytes 294920 | tf_op jit(solution)/shard_map/ppermute | solution.py:29
  17.0 2.2 %inner.1 = (f32[24,128]{1,0:T(8,128)S(1)}, f32[256,256]{1,0:T(8,128)S(1)}) custom-call(bf16[4,4,64,128]{3,2,1,0:T(8,128)(2,1)S(1)} %get-tuple-element.25.f_ref, bf16[1,4,64,128]{3,2,1,0:T(8,128)(2,1)S(1)} %collective-permute-done.yfar_ref, bf16[1,4,64,128]{3,2,1,0:T(8,128)(2,1)S(1)} %collective-permute-done.1.ynear_ref, ...), custom_call_target="tpu_custom_call" | custom-call | flops 2000000000 | bytes 1000000 | tf_op jit(solution)/shard_map/inner/pallas_call | solution.py:308
  19.3 0.0 collective-permute-done.2.zfar_ref
  19.3 0.1 collective-permute-done.3.znear_ref
  19.4 1.8 %outer.1 = (f32[48,128]{1,0:T(8,128)S(1)}, bf16[512,128]{1,0:T(8,128)(2,1)S(1)}) custom-call(bf16[4,4,64,128]{3,2,1,0:T(8,128)(2,1)S(1)} %get-tuple-element.25.f_ref, bf16[1,4,64,128]{3,2,1,0:T(8,128)(2,1)S(1)} %collective-permute-done.yfar_ref, bf16[1,4,64,128]{3,2,1,0:T(8,128)(2,1)S(1)} %collective-permute-done.1.ynear_ref, ...), custom_call_target="tpu_custom_call" | custom-call | tf_op jit(solution)/shard_map/outer/pallas_call | solution.py:321
  21.2 13.0 %all_to_all.16 = bf16[8,64,128]{2,1,0:T(8,128)(2,1)S(1)} all-to-all(bf16[8,64,128]{2,1,0:T(8,128)(2,1)S(1)} %bitcast.12), channel_id=1, replica_groups={{0,1,128,129,256,257,384,385},{2,3,130,131,258,259,386,387},{4,5,132,13..., dimensions={0} | all-to-all | bytes 262144 | tf_op jit(solution)/shard_map/all_to_all | solution.py:386
  34.1 23.2 %all_to_all.17 = f32[64,1,128]{2,1,0:T(1,128)S(1)} all-to-all(f32[64,1,128]{2,1,0:T(1,128)S(1)} %bitcast.14), channel_id=1, replica_groups={{0,2,4,6,8,10,12,14,16,18,20,22,24,26,28,30,32,34,36,38,40,42,44,46,48,..., dimensions={0} | all-to-all | bytes 65536 | tf_op jit(solution)/shard_map/all_to_all | solution.py:388
  57.3 0.6 %finish.1 = (f32[48,128]{1,0:T(8,128)}, f32[1,128]{1,0:T(1,128)}) custom-call(f32[48,128]{1,0:T(8,128)S(1)} %get-tuple-element.44.values_ref, f32[64,128]{1,0:T(8,128)S(1)} %bitcast.11), custom_call_target="tpu_custom_call" | custom-call | tf_op jit(solution)/shard_map/finish/pallas_call | solution.py:341
  (5 shorter events, 0.1 us)
Async XLA Ops:
  1.8 10.8 %collective-permute-start = (bf16[1,4,64,128]{3,2,1,0:T(8,128)(2,1)S(1)}, bf16[1,4,64,128]{3,2,1,0:T(8,128)(2,1)S(1)}, u32[]{:S(2)}, u32[]{:S(2)}) collective-permute-start(bf16[1,4,64,128]{3,2,1,0:T(8,128)(2,1)S(1)} %get-tuple-element.26), channel_id=1, source_target_pairs={{1,2},{2,1},{3,4},{4,3},{5,6},{6,5},{7,8},{8,7},{9,10},{10,9},{11,... | collective-permute-start | bytes 196616 | tf_op jit(solution)/shard_map/ppermute | solution.py:29
  7.2 5.4 %collective-permute-start.1 = (bf16[1,4,64,128]{3,2,1,0:T(8,128)(2,1)S(1)}, bf16[1,4,64,128]{3,2,1,0:T(8,128)(2,1)S(1)}, u32[]{:S(2)}, u32[]{:S(2)}) collective-permute-start(bf16[1,4,64,128]{3,2,1,0:T(8,128)(2,1)S(1)} %get-tuple-element.27), channel_id=1, source_target_pairs={{0,1},{1,0},{2,3},{3,2},{4,5},{5,4},{6,7},{7,6},{8,9},{9,8},{10,11... | collective-permute-start | bytes 196616 | tf_op jit(solution)/shard_map/ppermute | solution.py:29
  12.7 6.6 %collective-permute-start.2 = (bf16[6,1,64,128]{3,2,1,0:T(8,128)(2,1)S(1)}, bf16[6,1,64,128]{3,2,1,0:T(8,128)(2,1)S(1)}, u32[]{:S(2)}, u32[]{:S(2)}) collective-permute-start(bf16[6,1,64,128]{3,2,1,0:T(8,128)(2,1)S(1)} %pad_maximum_fusion), channel_id=1, source_target_pairs={{16,32},{32,16},{48,64},{64,48},{80,96},{96,80},{112,128},{128,112... | collective-permute-start | bytes 294920 | tf_op jit(solution)/shard_map/ppermute | solution.py:29
  13.4 6.0 %collective-permute-start.3 = (bf16[6,1,64,128]{3,2,1,0:T(8,128)(2,1)S(1)}, bf16[6,1,64,128]{3,2,1,0:T(8,128)(2,1)S(1)}, u32[]{:S(2)}, u32[]{:S(2)}) collective-permute-start(bf16[6,1,64,128]{3,2,1,0:T(8,128)(2,1)S(1)} %pad_maximum_fusion.1), channel_id=1, source_target_pairs={{0,16},{16,0},{32,48},{48,32},{64,80},{80,64},{96,112},{112,96},{1... | collective-permute-start | bytes 294920 | tf_op jit(solution)/shard_map/ppermute | solution.py:29

commit v6 on v5

--- a/solution.py
+++ b/solution.py
@@ -9,7 +9,7 @@
 BINS = 16
 CORE = 4
 TAPS = 3
-SMALL = 6
+SMALL = 5
 FULL = (0, 1, 2)
 VMEM_LIMIT = 32 * 1024 * 1024
 
@@ -80,7 +80,7 @@
 
 
 def prepare_kernel(
-    taps_hbm, cb_ref, hb_ref, hw_ref, ids_ref, bins_ref, map_ref, w_ref, bias_ref, off_ref, heads_ref, a_ref, col_ref,
+    taps_hbm, cb_ref, hb_ref, ids_ref, bins_ref, map_ref, w_ref, bias_ref, off_ref, a_ref, col_ref,
     row_ref, taps_ref, sem,
 ):
     fetch = pltpu.make_async_copy(taps_hbm, taps_ref, sem)
@@ -93,10 +93,6 @@
         w_ref[64 * dx : 64 * dx + 64, 640:1024] = rows[:, 192:]
     bias_ref[...] = column_of(cb_ref[...], 64)
     off_ref[...] = column_of(hb_ref[...], 8)
-    head = jnp.concatenate([hw_ref[...].astype(jnp.float32), jnp.zeros((5, 64), jnp.float32)], axis=0)
-    blank = jnp.zeros((8, 64), jnp.float32)
-    lines = [jnp.concatenate([head if u == v else blank for u in range(4)], axis=1) for v in range(4)]
-    heads_ref[...] = jnp.concatenate(lines, axis=0).astype(jnp.bfloat16)
 
 
 def lookup(ids_ref, bins_ref, map_ref, a_ref, col_ref, row_ref):
@@ -222,8 +218,12 @@
 
 
 def inner_kernel(
-    f_ref, yfar_ref, ynear_ref, w_ref, bias_ref, heads_ref, hb_ref, a_ref, col_ref, part_ref, counts_ref, g_ref, b_ref
+    f_ref, yfar_ref, ynear_ref, w_ref, bias_ref, hw_ref, hb_ref, a_ref, col_ref, part_ref, counts_ref, heads_ref, g_ref, b_ref
 ):
+    head = jnp.concatenate([hw_ref[...].astype(jnp.float32), jnp.zeros((5, 64), jnp.float32)], axis=0)
+    blank = jnp.zeros((8, 64), jnp.float32)
+    lines = [jnp.concatenate([head if u == v else blank for u in range(4)], axis=1) for v in range(4)]
+    heads_ref[...] = jnp.concatenate(lines, axis=0).astype(jnp.bfloat16)
     ylow, yhigh = edges(ynear_ref, yfar_ref, "xy")
 
     def cell(y, z):
@@ -293,10 +293,10 @@
         prepare_kernel,
         out_shape=(
             shape((192, 1024), jnp.bfloat16), shape((64, 128), jnp.float32), shape((8, 128), jnp.float32),
-            shape((32, 256), jnp.bfloat16), shape((256, 6144), jnp.bfloat16), shape((48, 128), jnp.float32),
+            shape((256, 6144), jnp.bfloat16), shape((48, 128), jnp.float32),
         ),
-        in_specs=[pl.BlockSpec(memory_space=pltpu.HBM)] + vmem(6),
-        out_specs=tuple(vmem(6)),
+        in_specs=[pl.BlockSpec(memory_space=pltpu.HBM)] + vmem(5),
+        out_specs=tuple(vmem(5)),
         scratch_shapes=[pltpu.VMEM((48, 128), jnp.float32), pltpu.VMEM(taps.shape, taps.dtype), pltpu.SemaphoreType.DMA(())],
         compiler_params=pltpu.CompilerParams(vmem_limit_bytes=VMEM_LIMIT),
         cost_estimate=pl.CostEstimate(flops=10**9, bytes_accessed=10**7, transcendentals=0),
@@ -307,9 +307,9 @@
 def inner(*operands):
     return pl.pallas_call(
         inner_kernel,
-        out_shape=(shape((24, 128), jnp.float32), shape((256, 256), jnp.float32)),
+        out_shape=(shape((24, 128), jnp.float32), shape((256, 256), jnp.float32), shape((32, 256), jnp.bfloat16)),
         in_specs=vmem(9),
-        out_specs=tuple(vmem(2)),
+        out_specs=tuple(vmem(3)),
         scratch_shapes=[pltpu.VMEM((6 * 192, 512), jnp.bfloat16), pltpu.VMEM((256, 3072), jnp.bfloat16)],
         compiler_params=pltpu.CompilerParams(vmem_limit_bytes=VMEM_LIMIT),
         cost_estimate=pl.CostEstimate(flops=2 * 10**9, bytes_accessed=10**6, transcendentals=0),
@@ -360,13 +360,13 @@
 
 def on_device(features, conv_w, conv_b, head_w, head_b, bins, edge_ids, owner_map):
     last = CORE - 1
-    cells, ynear, yfar, znear, zfar, ids, bins, owner_map, conv_b, head_b, head_w = arrange(
+    cells, ynear, yfar, znear, zfar, ids, bins, owner_map, conv_b, head_b = arrange(
         features.reshape(1024, 128), edge_ids.reshape(48, 128), bins.reshape(16, 128), owner_map.reshape(32, 128),
-        conv_b.reshape(1, 64), head_b.reshape(1, 3), head_w,
+        conv_b.reshape(1, 64), head_b.reshape(1, 3),
     )
     ynear, yfar = swaps("xy", ynear, yfar)
     taps = jnp.transpose(conv_w, (2, 3, 4, 0, 1))
-    weights, bias, offset, heads, owners, columns = prepare(taps, conv_b, head_b, head_w, ids, bins, owner_map)
+    weights, bias, offset, owners, columns = prepare(taps, conv_b, head_b, ids, bins, owner_map)
     yeven, zeven = is_even("xy"), is_even("gz")
     ylow, yhigh = jnp.where(yeven, yfar, ynear), jnp.where(yeven, ynear, yfar)
 
@@ -376,7 +376,7 @@
         return jnp.concatenate([low, face, high], axis=0)
 
     znear, zfar = swaps("gz", with_corners(znear, zeven), with_corners(zfar, jnp.logical_not(zeven)))
-    part, counts = inner(cells, yfar, ynear, weights, bias, heads, offset, owners, columns)
+    part, counts, heads = inner(cells, yfar, ynear, weights, bias, head_w, offset, owners, columns)
     blended, table = outer(
         cells, yfar, ynear, zfar, znear, weights, bias, heads, offset, owners, columns, part, counts
     )

time: 58.3 us -> 58.3 us (level)
  no operation moved by 1% of the time
where the time goes in v6:
time: 58.3 us; the launch traced here: 57.9 us
  blocking collectives  36.1 us (62%)
  starting transfers between devices  13.7 us (23%)
  Pallas kernels  7.06 us (12%)
  between operations  0.79 us (1%)
    all_to_all x1, blocking collectives, on_device(): lax.all_to_all(sums, every, 0, 0, tiled=True, axis_index_groups=groups(two))  23.2 us
    ppermute x4, starting transfers between devices, swaps(): return (lax.ppermute(inside, axis, near), lax.ppermute(outside, axis, far))  13.7 us
    all_to_all x1, blocking collectives, on_device(): lax.all_to_all(parts, every, 0, 0, tiled=True, axis_index_groups=groups(o...  13 us
    pallas_call x1, Pallas kernels, inner(): pl.pallas_call(inner_kernel, out_shape=(shape((24, 128), jnp.float32), sh...  2.22 us
    pallas_call x1, Pallas kernels, outer(): pl.pallas_call(outer_kernel, out_shape=(shape((48, 128), jnp.float32), sh...  1.75 us
    pallas_call x1, Pallas kernels, prepare(): pl.pallas_call(prepare_kernel, out_shape=(shape((192, 1024), jnp.bfloat16...  1.28 us
    pallas_call x1, Pallas kernels, arrange(): pl.pallas_call(arrange_kernel, out_shape=(shape((CORE, CORE, 64, 128), jn...  1.19 us
  transfers between devices with their start and end apart: 4, of which 1 were waited for; matrix products, arithmetic and copies ran while one was open for 0% of the time, Pallas kernels for 6%

profile of v6, /device:TPU:1, one launch (start us, length us, event | category | flops | bytes accessed | tf_op | source)
XLA Modules:
  0.0 57.9 jit_solution(3087439882684464585)
XLA Ops:
  0.6 0.0 copy-start
  0.6 1.2 %arrange.1 = (bf16[4,4,64,128]{3,2,1,0:T(8,128)(2,1)S(1)}, bf16[1,4,64,128]{3,2,1,0:T(8,128)(2,1)S(1)}, bf16[1,4,64,128]{3,2,1,0:T(8,128)(2,1)S(1)}, bf16[4,1,64...) custom-call(bf16[1024,128]{1,0:T(8,128)(2,1)} %bitcast.13, ...), custom_call_target="tpu_custom_call" | custom-call | tf_op jit(solution)/shard_map/arrange/pallas_call | solution.py:277
  1.8 5.4 %collective-permute-start = (bf16[1,4,64,128]{3,2,1,0:T(8,128)(2,1)S(1)}, bf16[1,4,64,128]{3,2,1,0:T(8,128)(2,1)S(1)}, u32[]{:S(2)}, u32[]{:S(2)}) collective-permute-start(bf16[1,4,64,128]{3,2,1,0:T(8,128)(2,1)S(1)} %get-tuple-element.25), channel_id=1, source_target_pairs={{1,2},{2,1},{3,4},{4,3},{5,6},{6,5},{7,8},{8,7},{9,10},{10,9},{11,... | collective-permute-start | bytes 196616 | tf_op jit(solution)/shard_map/ppermute | solution.py:29
  7.2 4.1 %collective-permute-start.1 = (bf16[1,4,64,128]{3,2,1,0:T(8,128)(2,1)S(1)}, bf16[1,4,64,128]{3,2,1,0:T(8,128)(2,1)S(1)}, u32[]{:S(2)}, u32[]{:S(2)}) collective-permute-start(bf16[1,4,64,128]{3,2,1,0:T(8,128)(2,1)S(1)} %get-tuple-element.26), channel_id=1, source_target_pairs={{0,1},{1,0},{2,3},{3,2},{4,5},{5,4},{6,7},{7,6},{8,9},{9,8},{10,11... | collective-permute-start | bytes 196616 | tf_op jit(solution)/shard_map/ppermute | solution.py:29
  11.3 1.3 %prepare.1 = (bf16[192,1024]{1,0:T(8,128)(2,1)S(1)}, f32[64,128]{1,0:T(8,128)S(1)}, f32[8,128]{1,0:T(8,128)S(1)}, bf16[256,6144]{1,0:T(8,128)(2,1)S(1)}, f32[48,128]{1,0:T(8,128)S(1)}) custom-call(bf16[3,3,3,64,64]{4,3,2,1,0:T(8,128)(2,1)} %bitcast.20, f32[1,64]{1,0:T(1,128)S(1)} %get-tuple-element.29.cb_ref, f32[1,3]{1,0:T(1,128)S(1)} %get-tuple-element.30.hb_ref, ...), custom_call_target="tpu_custom_call" | custom-call | flops 1000000000 | bytes 10000000 | tf_op jit(solution)/shard_map/prepare/pallas_call | solution.py:292
  12.6 0.0 collective-permute-done.yfar_ref
  12.6 0.0 collective-permute-done.1.ynear_ref
  12.7 0.7 %collective-permute-start.2 = (bf16[6,1,64,128]{3,2,1,0:T(8,128)(2,1)S(1)}, bf16[6,1,64,128]{3,2,1,0:T(8,128)(2,1)S(1)}, u32[]{:S(2)}, u32[]{:S(2)}) collective-permute-start(bf16[6,1,64,128]{3,2,1,0:T(8,128)(2,1)S(1)} %pad_maximum_fusion), channel_id=1, source_target_pairs={{16,32},{32,16},{48,64},{64,48},{80,96},{96,80},{112,128},{128,112... | collective-permute-start | bytes 294920 | tf_op jit(solution)/shard_map/ppermute | solution.py:29
  13.4 3.6 %collective-permute-start.3 = (bf16[6,1,64,128]{3,2,1,0:T(8,128)(2,1)S(1)}, bf16[6,1,64,128]{3,2,1,0:T(8,128)(2,1)S(1)}, u32[]{:S(2)}, u32[]{:S(2)}) collective-permute-start(bf16[6,1,64,128]{3,2,1,0:T(8,128)(2,1)S(1)} %pad_maximum_fusion.1), channel_id=1, source_target_pairs={{0,16},{16,0},{32,48},{48,32},{64,80},{80,64},{96,112},{112,96},{1... | collective-permute-start | bytes 294920 | tf_op jit(solution)/shard_map/ppermute | solution.py:29
  17.0 0.0 copy-done
  17.0 2.2 %inner.1 = (f32[24,128]{1,0:T(8,128)S(1)}, f32[256,256]{1,0:T(8,128)S(1)}, bf16[32,256]{1,0:T(8,128)(2,1)S(1)}) custom-call(bf16[4,4,64,128]{3,2,1,0:T(8,128)(2,1)S(1)} %get-tuple-element.24.f_ref, bf16[1,4,64,128]{3,2,1,0:T(8,128)(2,1)S(1)} %collective-permute-done.yfar_ref, bf16[1,4,64,128]{3,2,1,0:T(8,128)(2,1)S(1)} %collective-permute-done.1.ynear_ref, ...), custom_call_target="tpu_custom_call" | custom-call | flops 2000000000 | bytes 1000000 | tf_op jit(solution)/shard_map/inner/pallas_call | solution.py:308
  19.3 0.0 collective-permute-done.2.zfar_ref
  19.3 0.1 collective-permute-done.3.znear_ref
  19.4 1.8 %outer.1 = (f32[48,128]{1,0:T(8,128)S(1)}, bf16[512,128]{1,0:T(8,128)(2,1)S(1)}) custom-call(bf16[4,4,64,128]{3,2,1,0:T(8,128)(2,1)S(1)} %get-tuple-element.24.f_ref, bf16[1,4,64,128]{3,2,1,0:T(8,128)(2,1)S(1)} %collective-permute-done.yfar_ref, bf16[1,4,64,128]{3,2,1,0:T(8,128)(2,1)S(1)} %collective-permute-done.1.ynear_ref, ...), custom_call_target="tpu_custom_call" | custom-call | tf_op jit(solution)/shard_map/outer/pallas_call | solution.py:321
  21.2 13.0 %all_to_all.16 = bf16[8,64,128]{2,1,0:T(8,128)(2,1)S(1)} all-to-all(bf16[8,64,128]{2,1,0:T(8,128)(2,1)S(1)} %bitcast.12), channel_id=1, replica_groups={{0,1,128,129,256,257,384,385},{2,3,130,131,258,259,386,387},{4,5,132,13..., dimensions={0} | all-to-all | bytes 262144 | tf_op jit(solution)/shard_map/all_to_all | solution.py:386
  34.1 23.2 %all_to_all.17 = f32[64,1,128]{2,1,0:T(1,128)S(1)} all-to-all(f32[64,1,128]{2,1,0:T(1,128)S(1)} %bitcast.14), channel_id=1, replica_groups={{0,2,4,6,8,10,12,14,16,18,20,22,24,26,28,30,32,34,36,38,40,42,44,46,48,..., dimensions={0} | all-to-all | bytes 65536 | tf_op jit(solution)/shard_map/all_to_all | solution.py:388
  57.3 0.6 %finish.1 = (f32[48,128]{1,0:T(8,128)}, f32[1,128]{1,0:T(1,128)}) custom-call(f32[48,128]{1,0:T(8,128)S(1)} %get-tuple-element.42.values_ref, f32[64,128]{1,0:T(8,128)S(1)} %bitcast.11), custom_call_target="tpu_custom_call" | custom-call | tf_op jit(solution)/shard_map/finish/pallas_call | solution.py:341
  (5 shorter events, 0.1 us)
Async XLA Ops:
  0.6 16.4 %copy-start = (bf16[3,64]{1,0:T(4,128)(2,1)S(1)}, bf16[3,64]{1,0:T(4,128)(2,1)}, u32[]{:S(2)}) copy-start(bf16[3,64]{1,0:T(4,128)(2,1)} %hw_ref.1) | copy-start | bytes 1156
  1.8 10.8 %collective-permute-start = (bf16[1,4,64,128]{3,2,1,0:T(8,128)(2,1)S(1)}, bf16[1,4,64,128]{3,2,1,0:T(8,128)(2,1)S(1)}, u32[]{:S(2)}, u32[]{:S(2)}) collective-permute-start(bf16[1,4,64,128]{3,2,1,0:T(8,128)(2,1)S(1)} %get-tuple-element.25), channel_id=1, source_target_pairs={{1,2},{2,1},{3,4},{4,3},{5,6},{6,5},{7,8},{8,7},{9,10},{10,9},{11,... | collective-permute-start | bytes 196616 | tf_op jit(solution)/shard_map/ppermute | solution.py:29
  7.2 5.4 %collective-permute-start.1 = (bf16[1,4,64,128]{3,2,1,0:T(8,128)(2,1)S(1)}, bf16[1,4,64,128]{3,2,1,0:T(8,128)(2,1)S(1)}, u32[]{:S(2)}, u32[]{:S(2)}) collective-permute-start(bf16[1,4,64,128]{3,2,1,0:T(8,128)(2,1)S(1)} %get-tuple-element.26), channel_id=1, source_target_pairs={{0,1},{1,0},{2,3},{3,2},{4,5},{5,4},{6,7},{7,6},{8,9},{9,8},{10,11... | collective-permute-start | bytes 196616 | tf_op jit(solution)/shard_map/ppermute | solution.py:29
  12.7 6.6 %collective-permute-start.2 = (bf16[6,1,64,128]{3,2,1,0:T(8,128)(2,1)S(1)}, bf16[6,1,64,128]{3,2,1,0:T(8,128)(2,1)S(1)}, u32[]{:S(2)}, u32[]{:S(2)}) collective-permute-start(bf16[6,1,64,128]{3,2,1,0:T(8,128)(2,1)S(1)} %pad_maximum_fusion), channel_id=1, source_target_pairs={{16,32},{32,16},{48,64},{64,48},{80,96},{96,80},{112,128},{128,112... | collective-permute-start | bytes 294920 | tf_op jit(solution)/shard_map/ppermute | solution.py:29
  13.4 6.0 %collective-permute-start.3 = (bf16[6,1,64,128]{3,2,1,0:T(8,128)(2,1)S(1)}, bf16[6,1,64,128]{3,2,1,0:T(8,128)(2,1)S(1)}, u32[]{:S(2)}, u32[]{:S(2)}) collective-permute-start(bf16[6,1,64,128]{3,2,1,0:T(8,128)(2,1)S(1)} %pad_maximum_fusion.1), channel_id=1, source_target_pairs={{0,16},{16,0},{32,48},{48,32},{64,80},{80,64},{96,112},{112,96},{1... | collective-permute-start | bytes 294920 | tf_op jit(solution)/shard_map/ppermute | solution.py:29

commit v7 on v6

--- a/solution.py
+++ b/solution.py
@@ -80,7 +80,7 @@
 
 
 def prepare_kernel(
-    taps_hbm, cb_ref, hb_ref, ids_ref, bins_ref, map_ref, w_ref, bias_ref, off_ref, a_ref, col_ref,
+    taps_hbm, cb_ref, hb_ref, ids_ref, bins_ref, map_ref, w_ref, bias_ref, off_ref, a_ref, col_ref, edge_ref,
     row_ref, taps_ref, sem,
 ):
     fetch = pltpu.make_async_copy(taps_hbm, taps_ref, sem)
@@ -91,6 +91,7 @@
         rows = jnp.concatenate([taps_ref[t % 3, t // 3, dx] for t in range(9)], axis=1)
         w_ref[64 * dx : 64 * dx + 64, :576] = rows
         w_ref[64 * dx : 64 * dx + 64, 640:1024] = rows[:, 192:]
+        edge_ref[64 * dx : 64 * dx + 64] = jnp.concatenate([taps_ref[t % 2 * 2, t // 2, dx] for t in range(6)], axis=1)
     bias_ref[...] = column_of(cb_ref[...], 64)
     off_ref[...] = column_of(hb_ref[...], 8)
 
@@ -126,21 +127,40 @@
         a_ref[:, i * 128 : i * 128 + 128] = jnp.where(count == row, one, none)
 
 
-def predictions(zs, cell, w_ref, bias_ref, heads_ref, hb_ref, g_ref):
-    width = 128 * len(zs)
+def matmul(left, right):
+    return lax.dot_general(left, right, (((1,), (0,)), ((), ())), preferred_element_type=jnp.float32)
+
+
+def convolve(weight, rows):
+    yield 0, matmul(weight(0, 3), rows(0, 3))
+    cut = matmul(weight(0, 2), rows(1, 3))
+    yield 2, cut
+    yield 1, cut + matmul(weight(2, 3), rows(3, 4))
+    cut = matmul(weight(1, 3), rows(3, 5))
+    yield 3, cut
+    yield 4, cut + matmul(weight(0, 1), rows(2, 3))
+    yield 5, matmul(weight(0, 3), rows(3, 6))
+
+
+def whole(w_ref):
+    return lambda first, end: w_ref[:, first * 192 : end * 192] if first == 0 else w_ref[:, 448 + first * 192 : 448 + end * 192]
+
+
+def lay(zs, cell, g_ref, taps):
     zero = jnp.zeros((64, 128), jnp.bfloat16)
     for y in range(6):
-        for dz in range(TAPS):
+        for at, dz in enumerate(taps):
             for i, v in enumerate(zs):
                 z, kept = VARIANTS[v]
-                part = cell(y, z + dz) if dz in kept else zero
-                g_ref[(y * 3 + dz) * 64 : (y * 3 + dz) * 64 + 64, i * 128 : i * 128 + 128] = part
+                part = cell(y, z + dz) if dz in kept else None
+                first = (y * len(taps) + at) * 64
+                g_ref[first : first + 64, i * 128 : i * 128 + 128] = zero if part is None else part
+
+
+def predictions(zs, tiles, bias_ref, heads_ref, hb_ref):
     lane = lax.broadcasted_iota(jnp.int32, (64, 128), 1)
     bias = bias_ref[...]
     preds = {}
-
-    def matmul(left, right):
-        return lax.dot_general(left, right, (((1,), (0,)), ((), ())), preferred_element_type=jnp.float32)
 
     def activate(p):
         hidden = []
@@ -162,23 +182,12 @@
                 preds[zs[start // 128 + half], yv] = jax.nn.sigmoid(logit)
 
     batch = []
-    for start in range(0, width, 256):
-        cols = slice(start, start + 256)
-
-        def finish(yv, p):
-            batch.append((yv, start, activate(p)))
+    for tile, sums in enumerate(tiles):
+        for yv, p in sums:
+            batch.append((yv, tile * 256, activate(p)))
             if len(batch) == 4:
                 head(batch)
                 batch.clear()
-
-        finish(0, matmul(w_ref[:, :576], g_ref[:576, cols]))
-        cut = matmul(w_ref[:, :384], g_ref[192:576, cols])
-        finish(2, cut)
-        finish(1, cut + matmul(w_ref[:, 832:1024], g_ref[576:768, cols]))
-        cut = matmul(w_ref[:, 640:1024], g_ref[576:960, cols])
-        finish(3, cut)
-        finish(4, cut + matmul(w_ref[:, :192], g_ref[384:576, cols]))
-        finish(5, matmul(w_ref[:, :576], g_ref[576:1152, cols]))
     if batch:
         head(batch)
     return preds
@@ -218,7 +227,8 @@
 
 
 def inner_kernel(
-    f_ref, yfar_ref, ynear_ref, w_ref, bias_ref, hw_ref, hb_ref, a_ref, col_ref, part_ref, counts_ref, heads_ref, g_ref, b_ref
+    f_ref, yfar_ref, ynear_ref, w_ref, bias_ref, hw_ref, hb_ref, a_ref, col_ref, part_ref, counts_ref, heads_ref, own_ref,
+    g_ref, b_ref, h_ref,
 ):
     head = jnp.concatenate([hw_ref[...].astype(jnp.float32), jnp.zeros((5, 64), jnp.float32)], axis=0)
     blank = jnp.zeros((8, 64), jnp.float32)
@@ -229,25 +239,37 @@
     def cell(y, z):
         return ylow(0, z - 1) if y == 0 else (yhigh(0, z - 1) if y == 5 else f_ref[y - 1, z - 1])
 
-    blends = blend(predictions(INNER, cell, w_ref, bias_ref, heads_ref, hb_ref, g_ref))
+    def own(y, z):
+        return None if z in (0, 5) else cell(y, z)
+
+    lay(INNER, cell, g_ref, FULL)
+    tiles = [
+        convolve(whole(w_ref), lambda first, end, at=at: g_ref[first * 192 : end * 192, at : at + 256]) for at in (0, 256)
+    ]
+    blends = blend(predictions(INNER, tiles, bias_ref, heads_ref, hb_ref))
+    lay(OUTER, own, h_ref, FULL)
+    for yv, p in convolve(whole(w_ref), lambda first, end: h_ref[first * 192 : end * 192]):
+        own_ref[yv] = p
     for i, (axis, at) in enumerate(INNER_ROWS):
         part_ref[i : i + 1] = blends[at][axis : axis + 1]
     counts_ref[...] = histogram(INNER_ROWS, part_ref, col_ref, a_ref[:, : 24 * 128], b_ref)
 
 
 def outer_kernel(
-    f_ref, yfar_ref, ynear_ref, zfar_ref, znear_ref, w_ref, bias_ref, heads_ref, hb_ref, a_ref, col_ref, part_ref, counts_ref,
+    znear_ref, zfar_ref, w_ref, bias_ref, heads_ref, hb_ref, a_ref, col_ref, part_ref, counts_ref, own_ref,
     out_ref, table_ref, g_ref, b_ref, value_ref,
 ):
-    ylow, yhigh = edges(ynear_ref, yfar_ref, "xy")
     zlow, zhigh = edges(znear_ref, zfar_ref, "gz")
 
-    def cell(y, z):
-        if z == 0 or z == 5:
-            return (zlow if z == 0 else zhigh)(y, 0)
-        return ylow(0, z - 1) if y == 0 else (yhigh(0, z - 1) if y == 5 else f_ref[y - 1, z - 1])
-
-    blends = blend(predictions(OUTER, cell, w_ref, bias_ref, heads_ref, hb_ref, g_ref))
+    def halo(y, z):
+        return zlow(y, 0) if z == 0 else (zhigh(y, 0) if z == 5 else None)
+
+    lay(OUTER, halo, g_ref, (0, 2))
+    sums = convolve(
+        lambda first, end: w_ref[:, first * 128 : end * 128], lambda first, end: g_ref[first * 128 : end * 128]
+    )
+    tiles = [((yv, p + own_ref[yv]) for yv, p in sums)]
+    blends = blend(predictions(OUTER, tiles, bias_ref, heads_ref, hb_ref))
     for i, (axis, at) in enumerate(OUTER_ROWS):
         value_ref[i : i + 1] = blends[at][axis : axis + 1]
     for axis in range(3):
@@ -293,10 +315,10 @@
         prepare_kernel,
         out_shape=(
             shape((192, 1024), jnp.bfloat16), shape((64, 128), jnp.float32), shape((8, 128), jnp.float32),
-            shape((256, 6144), jnp.bfloat16), shape((48, 128), jnp.float32),
+            shape((256, 6144), jnp.bfloat16), shape((48, 128), jnp.float32), shape((192, 384), jnp.bfloat16),
         ),
         in_specs=[pl.BlockSpec(memory_space=pltpu.HBM)] + vmem(5),
-        out_specs=tuple(vmem(5)),
+        out_specs=tuple(vmem(6)),
         scratch_shapes=[pltpu.VMEM((48, 128), jnp.float32), pltpu.VMEM(taps.shape, taps.dtype), pltpu.SemaphoreType.DMA(())],
         compiler_params=pltpu.CompilerParams(vmem_limit_bytes=VMEM_LIMIT),
         cost_estimate=pl.CostEstimate(flops=10**9, bytes_accessed=10**7, transcendentals=0),
@@ -307,10 +329,10 @@
 def inner(*operands):
     return pl.pallas_call(
         inner_kernel,
-        out_shape=(shape((24, 128), jnp.float32), shape((256, 256), jnp.float32), shape((32, 256), jnp.bfloat16)),
+        out_shape=(shape((24, 128), jnp.float32), shape((256, 256), jnp.float32), shape((32, 256), jnp.bfloat16), shape((6, 192, 256), jnp.float32)),
         in_specs=vmem(9),
-        out_specs=tuple(vmem(3)),
-        scratch_shapes=[pltpu.VMEM((6 * 192, 512), jnp.bfloat16), pltpu.VMEM((256, 3072), jnp.bfloat16)],
+        out_specs=tuple(vmem(4)),
+        scratch_shapes=[pltpu.VMEM((6 * 192, 512), jnp.bfloat16), pltpu.VMEM((256, 3072), jnp.bfloat16), pltpu.VMEM((6 * 192, 256), jnp.bfloat16)],
         compiler_params=pltpu.CompilerParams(vmem_limit_bytes=VMEM_LIMIT),
         cost_estimate=pl.CostEstimate(flops=2 * 10**9, bytes_accessed=10**6, transcendentals=0),
         name="inner",
@@ -321,10 +343,10 @@
     return pl.pallas_call(
         outer_kernel,
         out_shape=(shape((48, 128), jnp.float32), shape((512, 128), jnp.bfloat16)),
-        in_specs=vmem(13),
+        in_specs=vmem(11),
         out_specs=tuple(vmem(2)),
         scratch_shapes=[
-            pltpu.VMEM((6 * 192, 256), jnp.bfloat16), pltpu.VMEM((256, 3072), jnp.bfloat16),
+            pltpu.VMEM((6 * 128, 256), jnp.bfloat16), pltpu.VMEM((256, 3072), jnp.bfloat16),
             pltpu.VMEM((24, 128), jnp.float32),
         ],
         compiler_params=pltpu.CompilerParams(vmem_limit_bytes=VMEM_LIMIT),
@@ -366,7 +388,7 @@
     )
     ynear, yfar = swaps("xy", ynear, yfar)
     taps = jnp.transpose(conv_w, (2, 3, 4, 0, 1))
-    weights, bias, offset, owners, columns = prepare(taps, conv_b, head_b, ids, bins, owner_map)
+    weights, bias, offset, owners, columns, halo_weights = prepare(taps, conv_b, head_b, ids, bins, owner_map)
     yeven, zeven = is_even("xy"), is_even("gz")
     ylow, yhigh = jnp.where(yeven, yfar, ynear), jnp.where(yeven, ynear, yfar)
 
@@ -376,9 +398,9 @@
         return jnp.concatenate([low, face, high], axis=0)
 
     znear, zfar = swaps("gz", with_corners(znear, zeven), with_corners(zfar, jnp.logical_not(zeven)))
-    part, counts, heads = inner(cells, yfar, ynear, weights, bias, head_w, offset, owners, columns)
+    part, counts, heads, own = inner(cells, yfar, ynear, weights, bias, head_w, offset, owners, columns)
     blended, table = outer(
-        cells, yfar, ynear, zfar, znear, weights, bias, heads, offset, owners, columns, part, counts
+        znear, zfar, halo_weights, bias, heads, offset, owners, columns, part, counts, own
     )
     every = ("gz", "xy")
     one, two = EXCHANGES

time: 58.3 us -> 58.2 us (level)
  transfers between devices with their start and end apart: 4 -> 4, of which waited for: 1 -> 0; matrix products, arithmetic and copies ran while one was open for 0% -> 0% of each run, Pallas kernels for 6% -> 7%
where the time goes in v7:
time: 58.2 us; the launch traced here: 57.8 us
  blocking collectives  35.9 us (62%)
  starting transfers between devices  13.7 us (24%)
  Pallas kernels  7.3 us (13%)
  between operations  0.8 us (1%)
    all_to_all x1, blocking collectives, on_device(): lax.all_to_all(sums, every, 0, 0, tiled=True, axis_index_groups=groups(two))  23.1 us
    ppermute x4, starting transfers between devices, swaps(): return (lax.ppermute(inside, axis, near), lax.ppermute(outside, axis, far))  13.7 us
    all_to_all x1, blocking collectives, on_device(): lax.all_to_all(parts, every, 0, 0, tiled=True, axis_index_groups=groups(o...  12.8 us
    pallas_call x1, Pallas kernels, inner(): pl.pallas_call(inner_kernel, out_shape=(shape((24, 128), jnp.float32), sh...  2.53 us
    pallas_call x1, Pallas kernels, outer(): pl.pallas_call(outer_kernel, out_shape=(shape((48, 128), jnp.float32), sh...  1.58 us
    pallas_call x1, Pallas kernels, prepare(): pl.pallas_call(prepare_kernel, out_shape=(shape((192, 1024), jnp.bfloat16...  1.39 us
    pallas_call x1, Pallas kernels, arrange(): pl.pallas_call(arrange_kernel, out_shape=(shape((CORE, CORE, 64, 128), jn...  1.19 us
  transfers between devices with their start and end apart: 4, of which 0 were waited for; matrix products, arithmetic and copies ran while one was open for 0% of the time, Pallas kernels for 7%

profile of v7, /device:TPU:1, one launch (start us, length us, event | category | flops | bytes accessed | tf_op | source)
XLA Modules:
  0.0 57.8 jit_solution(10885388696957514175)
XLA Ops:
  0.6 0.0 copy-start
  0.6 1.2 %arrange.1 = (bf16[4,4,64,128]{3,2,1,0:T(8,128)(2,1)S(1)}, bf16[1,4,64,128]{3,2,1,0:T(8,128)(2,1)S(1)}, bf16[1,4,64,128]{3,2,1,0:T(8,128)(2,1)S(1)}, bf16[4,1,64...) custom-call(bf16[1024,128]{1,0:T(8,128)(2,1)} %bitcast.13, ...), custom_call_target="tpu_custom_call" | custom-call | tf_op jit(solution)/shard_map/arrange/pallas_call | solution.py:299
  1.8 5.4 %collective-permute-start = (bf16[1,4,64,128]{3,2,1,0:T(8,128)(2,1)S(1)}, bf16[1,4,64,128]{3,2,1,0:T(8,128)(2,1)S(1)}, u32[]{:S(2)}, u32[]{:S(2)}) collective-permute-start(bf16[1,4,64,128]{3,2,1,0:T(8,128)(2,1)S(1)} %get-tuple-element.26), channel_id=1, source_target_pairs={{1,2},{2,1},{3,4},{4,3},{5,6},{6,5},{7,8},{8,7},{9,10},{10,9},{11,... | collective-permute-start | bytes 196616 | tf_op jit(solution)/shard_map/ppermute | solution.py:29
  7.2 4.1 %collective-permute-start.1 = (bf16[1,4,64,128]{3,2,1,0:T(8,128)(2,1)S(1)}, bf16[1,4,64,128]{3,2,1,0:T(8,128)(2,1)S(1)}, u32[]{:S(2)}, u32[]{:S(2)}) collective-permute-start(bf16[1,4,64,128]{3,2,1,0:T(8,128)(2,1)S(1)} %get-tuple-element.27), channel_id=1, source_target_pairs={{0,1},{1,0},{2,3},{3,2},{4,5},{5,4},{6,7},{7,6},{8,9},{9,8},{10,11... | collective-permute-start | bytes 196616 | tf_op jit(solution)/shard_map/ppermute | solution.py:29
  11.3 1.4 %prepare.1 = (bf16[192,1024]{1,0:T(8,128)(2,1)S(1)}, f32[64,128]{1,0:T(8,128)S(1)}, f32[8,128]{1,0:T(8,128)S(1)}, bf16[256,6144]{1,0:T(8,128)(2,1)S(1)}, f32[48,...) custom-call(bf16[3,3,3,64,64]{4,3,2,1,0:T(8,128)(2,1)} %bitcast.20, f32[1,64]{1,0:T(1,128)S(1)} %get-tuple-element.30.cb_ref, ...), custom_call_target="tpu_custom_call" | custom-call | flops 1000000000 | bytes 10000000 | tf_op jit(solution)/shard_map/prepare/pallas_call | solution.py:314
  12.7 0.0 collective-permute-done.yfar_ref
  12.7 0.0 collective-permute-done.1.ynear_ref
  12.8 0.7 %collective-permute-start.3 = (bf16[6,1,64,128]{3,2,1,0:T(8,128)(2,1)S(1)}, bf16[6,1,64,128]{3,2,1,0:T(8,128)(2,1)S(1)}, u32[]{:S(2)}, u32[]{:S(2)}) collective-permute-start(bf16[6,1,64,128]{3,2,1,0:T(8,128)(2,1)S(1)} %pad_maximum_fusion.1), channel_id=1, source_target_pairs={{16,32},{32,16},{48,64},{64,48},{80,96},{96,80},{112,128},{128,112... | collective-permute-start | bytes 294920 | tf_op jit(solution)/shard_map/ppermute | solution.py:29
  13.5 3.6 %collective-permute-start.2 = (bf16[6,1,64,128]{3,2,1,0:T(8,128)(2,1)S(1)}, bf16[6,1,64,128]{3,2,1,0:T(8,128)(2,1)S(1)}, u32[]{:S(2)}, u32[]{:S(2)}) collective-permute-start(bf16[6,1,64,128]{3,2,1,0:T(8,128)(2,1)S(1)} %pad_maximum_fusion), channel_id=1, source_target_pairs={{0,16},{16,0},{32,48},{48,32},{64,80},{80,64},{96,112},{112,96},{1... | collective-permute-start | bytes 294920 | tf_op jit(solution)/shard_map/ppermute | solution.py:29
  17.1 0.0 copy-done
  17.1 2.5 %inner.1 = (f32[24,128]{1,0:T(8,128)S(1)}, f32[256,256]{1,0:T(8,128)S(1)}, bf16[32,256]{1,0:T(8,128)(2,1)S(1)}, f32[6,192,256]{2,1,0:T(8,128)S(1)}) custom-call(bf16[4,4,64,128]{3,2,1,0:T(8,128)(2,1)S(1)} %get-tuple-element.37.f_ref, bf16[1,4,64,128]{3,2,1,0:T(8,128)(2,1)S(1)} %collective-permute-done.yfar_ref, ...), custom_call_target="tpu_custom_call" | custom-call | flops 2000000000 | bytes 1000000 | tf_op jit(solution)/shard_map/inner/pallas_call | solution.py:330
  19.7 0.0 collective-permute-done.3.zfar_ref
  19.7 0.0 collective-permute-done.2.znear_ref
  19.7 1.6 %outer.1 = (f32[48,128]{1,0:T(8,128)S(1)}, bf16[512,128]{1,0:T(8,128)(2,1)S(1)}) custom-call(bf16[6,1,64,128]{3,2,1,0:T(8,128)(2,1)S(1)} %collective-permute-done.2.znear_ref, bf16[6,1,64,128]{3,2,1,0:T(8,128)(2,1)S(1)} %collective-permute-done.3.zfar_ref, bf16[192,384]{1,0:T(8,128)(2,1)S(1)} %get-tuple-element.35.w_ref, ...), custom_call_target="tpu_custom_call" | custom-call | tf_op jit(solution)/shard_map/outer/pallas_call | solution.py:343
  21.3 12.8 %all_to_all.16 = bf16[8,64,128]{2,1,0:T(8,128)(2,1)S(1)} all-to-all(bf16[8,64,128]{2,1,0:T(8,128)(2,1)S(1)} %bitcast.12), channel_id=1, replica_groups={{0,1,128,129,256,257,384,385},{2,3,130,131,258,259,386,387},{4,5,132,13..., dimensions={0} | all-to-all | bytes 262144 | tf_op jit(solution)/shard_map/all_to_all | solution.py:408
  34.1 23.1 %all_to_all.17 = f32[64,1,128]{2,1,0:T(1,128)S(1)} all-to-all(f32[64,1,128]{2,1,0:T(1,128)S(1)} %bitcast.14), channel_id=1, replica_groups={{0,2,4,6,8,10,12,14,16,18,20,22,24,26,28,30,32,34,36,38,40,42,44,46,48,..., dimensions={0} | all-to-all | bytes 65536 | tf_op jit(solution)/shard_map/all_to_all | solution.py:410
  57.2 0.6 %finish.1 = (f32[48,128]{1,0:T(8,128)}, f32[1,128]{1,0:T(1,128)}) custom-call(f32[48,128]{1,0:T(8,128)S(1)} %get-tuple-element.46.values_ref, f32[64,128]{1,0:T(8,128)S(1)} %bitcast.11), custom_call_target="tpu_custom_call" | custom-call | tf_op jit(solution)/shard_map/finish/pallas_call | solution.py:363
  (5 shorter events, 0.1 us)
Async XLA Ops:
  0.6 16.5 %copy-start = (bf16[3,64]{1,0:T(4,128)(2,1)S(1)}, bf16[3,64]{1,0:T(4,128)(2,1)}, u32[]{:S(2)}) copy-start(bf16[3,64]{1,0:T(4,128)(2,1)} %hw_ref.1) | copy-start | bytes 1156
  1.8 10.9 %collective-permute-start = (bf16[1,4,64,128]{3,2,1,0:T(8,128)(2,1)S(1)}, bf16[1,4,64,128]{3,2,1,0:T(8,128)(2,1)S(1)}, u32[]{:S(2)}, u32[]{:S(2)}) collective-permute-start(bf16[1,4,64,128]{3,2,1,0:T(8,128)(2,1)S(1)} %get-tuple-element.26), channel_id=1, source_target_pairs={{1,2},{2,1},{3,4},{4,3},{5,6},{6,5},{7,8},{8,7},{9,10},{10,9},{11,... | collective-permute-start | bytes 196616 | tf_op jit(solution)/shard_map/ppermute | solution.py:29
  7.2 5.5 %collective-permute-start.1 = (bf16[1,4,64,128]{3,2,1,0:T(8,128)(2,1)S(1)}, bf16[1,4,64,128]{3,2,1,0:T(8,128)(2,1)S(1)}, u32[]{:S(2)}, u32[]{:S(2)}) collective-permute-start(bf16[1,4,64,128]{3,2,1,0:T(8,128)(2,1)S(1)} %get-tuple-element.27), channel_id=1, source_target_pairs={{0,1},{1,0},{2,3},{3,2},{4,5},{5,4},{6,7},{7,6},{8,9},{9,8},{10,11... | collective-permute-start | bytes 196616 | tf_op jit(solution)/shard_map/ppermute | solution.py:29
  12.8 6.9 %collective-permute-start.3 = (bf16[6,1,64,128]{3,2,1,0:T(8,128)(2,1)S(1)}, bf16[6,1,64,128]{3,2,1,0:T(8,128)(2,1)S(1)}, u32[]{:S(2)}, u32[]{:S(2)}) collective-permute-start(bf16[6,1,64,128]{3,2,1,0:T(8,128)(2,1)S(1)} %pad_maximum_fusion.1), channel_id=1, source_target_pairs={{16,32},{32,16},{48,64},{64,48},{80,96},{96,80},{112,128},{128,112... | collective-permute-start | bytes 294920 | tf_op jit(solution)/shard_map/ppermute | solution.py:29
  13.5 6.2 %collective-permute-start.2 = (bf16[6,1,64,128]{3,2,1,0:T(8,128)(2,1)S(1)}, bf16[6,1,64,128]{3,2,1,0:T(8,128)(2,1)S(1)}, u32[]{:S(2)}, u32[]{:S(2)}) collective-permute-start(bf16[6,1,64,128]{3,2,1,0:T(8,128)(2,1)S(1)} %pad_maximum_fusion), channel_id=1, source_target_pairs={{0,16},{16,0},{32,48},{48,32},{64,80},{80,64},{96,112},{112,96},{1... | collective-permute-start | bytes 294920 | tf_op jit(solution)/shard_map/ppermute | solution.py:29
